TPU v7x, 512 devices: a whole 4x8x8 slice. The times are simulated.
512 devices in a mesh: dp: 16 (over x_lo, y), ctx: 32 (over x_hi, z, core).
Axes of the slice: x: 4 (x_hi: 2, x_lo: 2; x = x_hi * 2 + x_lo), y: 8, z: 8, core: 2. Of those that a mesh axis runs over, the one named last changes fastest.
Arguments:
- queries: bfloat16 [16, 4096, 1024], P('dp', 'ctx'), may hold values from -6 to 6
- key_states: bfloat16 [16, 4096, 128], P('dp', 'ctx'), may hold values from -6 to 6
- value_states: bfloat16 [16, 4096, 128], P('dp', 'ctx'), may hold values from -6 to 6
- doc_start: int32 [16, 4096], P('dp', 'ctx'), may hold values from 0 to 4095, as said below
- move_plan: int32 [32, 8], P('ctx'), may hold values from 0 to 15, as said below
- out_grad: bfloat16 [16, 4096, 1024], P('dp', 'ctx'), may hold values from -6 to 6
Outputs:
- attn_moved: bfloat16 [16, 4096, 1024], P('dp', 'ctx')
- query_grad: bfloat16 [16, 4096, 1024], P('dp', 'ctx')
- key_grad: bfloat16 [16, 4096, 128], P('dp', 'ctx')
- value_grad: bfloat16 [16, 4096, 128], P('dp', 'ctx')
Inputs may be any that keep to these rules, and one draw needn't show every extreme that they name: doc_start[g, 0] = 0; doc_start[g, i] <= i; doc_start[g, i] is either i or doc_start[g, i - 1]. `move_plan`: the 8 values of each row are distinct.
All inputs are finite; a program needn't handle non-finite values.
Results may differ from a plain program's by a relative error of at most 0.03.
Values may be sent and summed in bfloat16 or wider, within the bound.
A program may use at most 64 MiB of HBM per device.

v0:
```python
import math

import jax
import jax.numpy as jnp
from jax import lax
from jax.sharding import PartitionSpec as P

HEADS = 8
HDIM = 128


MASKED_SCORE = -1e30


def over_tiles(tile_fn, running, key_rows, value_rows, key_first, tile_rows):
    total_rows = key_rows.shape[0]
    full_tiles = total_rows // tile_rows

    def tile_step(tile_index, current):
        offset = tile_index * tile_rows
        key_tile = lax.dynamic_slice_in_dim(key_rows, offset, tile_rows, 0)
        value_tile = lax.dynamic_slice_in_dim(value_rows, offset, tile_rows, 0)
        return tile_fn(current, key_tile, value_tile, key_first + offset)

    running = lax.fori_loop(0, full_tiles, tile_step, running)
    return running


def per_device(queries, key_states, value_states, doc_start, move_plan, out_grad):
    tok_rows = queries.shape[1]
    groups = lax.axis_size("dp")
    group_index = lax.axis_index("dp")
    ctx_index = lax.axis_index("ctx")
    seq_len = tok_rows * lax.axis_size("ctx")
    slot_count = move_plan.shape[1]
    block_rows = tok_rows // slot_count
    tile_rows = 4 * tok_rows
    score_scale = 1.0 / math.sqrt(HDIM)
    head_rows = tok_rows * HEADS
    query_rows = queries[0].reshape(head_rows, HDIM)
    positions = ctx_index * tok_rows + jnp.arange(tok_rows, dtype=jnp.int32)
    starts = doc_start[0]
    shifts = move_plan[0]
    ahead_ids = jnp.mod(group_index + shifts, groups)
    behind = jnp.mod(group_index - shifts, groups)
    group_ids = jnp.arange(groups, dtype=jnp.int32)

    def to_slots(source_rows, target):
        blocks = source_rows.reshape(slot_count, block_rows, source_rows.shape[1])
        onehot = (target[None, :] == group_ids[:, None]).astype(source_rows.dtype)
        placed = jnp.einsum("gs,sbw->gbw", onehot, blocks, preferred_element_type=jnp.float32)
        return placed.astype(source_rows.dtype)

    def from_slots(arrived, source):
        onehot = (source[:, None] == group_ids[None, :]).astype(arrived.dtype)
        placed = jnp.einsum("sg,gbw->sbw", onehot, arrived, preferred_element_type=jnp.float32)
        return placed.astype(arrived.dtype).reshape(tok_rows, arrived.shape[2])

    def scores(key_tile, key_first):
        key_count = key_tile.shape[0]
        raw_scores = (
            jnp.einsum("rd,nd->rn", query_rows, key_tile, preferred_element_type=jnp.float32)
            * score_scale
        )
        raw_scores = raw_scores.reshape(tok_rows, HEADS, key_count)
        key_pos = key_first + jnp.arange(key_count, dtype=jnp.int32)
        visible = (key_pos[None, :] >= starts[:, None]) & (key_pos[None, :] <= positions[:, None])
        return jnp.where(visible[:, None, :], raw_scores, MASKED_SCORE)

    def guarded(key_first, key_count, update, running):
        key_last = key_first + key_count - 1
        needed = jnp.any((key_first <= positions) & (key_last >= starts))
        return lax.cond(needed, update, lambda unused: unused, running)

    def stats_tile(running, key_tile, value_tile, key_first):

        def update(current):
            row_max, row_total = current
            masked = scores(key_tile, key_first)
            new_max = jnp.maximum(row_max, jnp.max(masked, axis=2))
            new_total = row_total * jnp.exp(row_max - new_max) + jnp.sum(
                jnp.exp(masked - new_max[:, :, None]), axis=2
            )
            return (new_max, new_total)

        return guarded(key_first, key_tile.shape[0], update, running)

    arrived_grad = lax.all_to_all(
        to_slots(out_grad[0], behind), "dp", split_axis=0, concat_axis=0, tiled=True
    )
    home_grad = from_slots(arrived_grad, ahead_ids)
    start_stats = (
        jnp.full((tok_rows, HEADS), MASKED_SCORE, jnp.float32),
        jnp.zeros((tok_rows, HEADS), jnp.float32),
    )
    key_piece = lax.all_gather(key_states[0], "ctx", axis=0, tiled=True)
    gathered = over_tiles(stats_tile, start_stats, key_piece, key_piece, jnp.int32(0), tile_rows)
    row_max = gathered[0]
    row_total = gathered[1]

    def output_tile(running, key_tile, value_tile, key_first):

        def update(current):
            masked = scores(key_tile, key_first)
            weights = (jnp.exp(masked - row_max[:, :, None]) / row_total[:, :, None]).astype(
                jnp.bfloat16
            )
            weights = weights.reshape(head_rows, key_tile.shape[0])
            return current + jnp.dot(weights, value_tile, preferred_element_type=jnp.float32)

        return guarded(key_first, key_tile.shape[0], update, running)

    zero_rows = jnp.zeros((head_rows, HDIM), jnp.float32)
    attended = over_tiles(
        output_tile,
        zero_rows,
        lax.all_gather(key_states[0], "ctx", axis=0, tiled=True),
        lax.all_gather(value_states[0], "ctx", axis=0, tiled=True),
        jnp.int32(0),
        tile_rows,
    )
    attn_rows = attended.astype(jnp.bfloat16).reshape(tok_rows, HEADS * HDIM)
    arrived_out = lax.all_to_all(
        to_slots(attn_rows, ahead_ids), "dp", split_axis=0, concat_axis=0, tiled=True
    )
    moved_out = from_slots(arrived_out, behind)
    grad_rows = home_grad.reshape(head_rows, HDIM)
    grad_heads = home_grad.reshape(tok_rows, HEADS, HDIM).astype(jnp.float32)
    grad_dot = jnp.sum(
        grad_heads * attn_rows.reshape(tok_rows, HEADS, HDIM).astype(jnp.float32), axis=2
    ).reshape(head_rows)
    full_keys, full_values = (
        lax.all_gather(key_states[0], "ctx", axis=0, tiled=True),
        lax.all_gather(value_states[0], "ctx", axis=0, tiled=True),
    )

    def backward_tile(running, key_tile, value_tile, key_first):
        key_count = key_tile.shape[0]

        def update(current):
            query_sum, pair_buffer = current
            masked = scores(key_tile, key_first)
            weights = (jnp.exp(masked - row_max[:, :, None]) / row_total[:, :, None]).reshape(
                head_rows, key_count
            )
            grad_weights = jnp.einsum(
                "rd,nd->rn", grad_rows, value_tile, preferred_element_type=jnp.float32
            )
            grad_scores = (weights * (grad_weights - grad_dot[:, None]) * score_scale).astype(
                jnp.bfloat16
            )
            query_sum = query_sum + jnp.dot(
                grad_scores, key_tile, preferred_element_type=jnp.float32
            )
            key_part = jnp.einsum(
                "rn,rd->nd", grad_scores, query_rows, preferred_element_type=jnp.float32
            )
            value_part = jnp.einsum(
                "rn,rd->nd",
                weights.astype(jnp.bfloat16),
                grad_rows,
                preferred_element_type=jnp.float32,
            )
            both_parts = jnp.concatenate([key_part, value_part], axis=1)
            pair_buffer = lax.dynamic_update_slice_in_dim(pair_buffer, both_parts, key_first, 0)
            return (query_sum, pair_buffer)

        return guarded(key_first, key_count, update, running)

    start_back = (zero_rows, jnp.zeros((seq_len, 2 * HDIM), jnp.float32))
    query_total, pair_buffer = over_tiles(
        backward_tile, start_back, full_keys, full_values, 0, tile_rows
    )
    summed = lax.psum_scatter(
        pair_buffer.astype(jnp.bfloat16), "ctx", scatter_dimension=0, tiled=True
    ).astype(jnp.float32)
    key_grad = summed[:, :HDIM].astype(jnp.bfloat16)
    value_grad = summed[:, HDIM:].astype(jnp.bfloat16)
    query_grad = query_total.astype(jnp.bfloat16).reshape(tok_rows, HEADS * HDIM)
    return (moved_out[None], query_grad[None], key_grad[None], value_grad[None])


def solution(mesh):
    placed = (
        P("dp", "ctx", None),
        P("dp", "ctx", None),
        P("dp", "ctx", None),
        P("dp", "ctx"),
        P("ctx", None),
        P("dp", "ctx", None),
    )
    return jax.shard_map(
        per_device,
        mesh=mesh,
        in_specs=placed,
        out_specs=(
            P("dp", "ctx", None),
            P("dp", "ctx", None),
            P("dp", "ctx", None),
            P("dp", "ctx", None),
        ),
        check_vma=False,
    )
```

profile of v0, /device:TPU:1, one launch (start us, length us, event | category | flops | bytes accessed | tf_op | source)
XLA Modules:
  0.0 425.7 jit_solution(17162291831110751274)
XLA Ops:
  7.2 0.7 all-gather.5.cloned.1.call-update
  7.9 1.2 fusion.55
  9.5 1.1 copy.37
  10.7 8.7 %all-to-all-start.1 = ((bf16[16,16,1024]{2,1,0:T(8,128)(2,1)}), bf16[16,16,1024]{2,1,0:T(8,128)(2,1)S(1)}, u32[]{:S(2)}, u32[]{:S(2)}) async-start(bf16[16,16,1024]{2,1,0:T(8,128)(2,1)} %copy.37), calls=%async_computation.1 | async-start | bytes 1048576 | tf_op jit(solution)/shard_map/all_to_all | solution.py:88
  19.4 0.7 all-gather.7.cloned.1.call-update
  20.8 11.7 %all-to-all-done.1 = bf16[16,16,1024]{2,1,0:T(8,128)(2,1)S(1)} async-done(((bf16[16,16,1024]{2,1,0:T(8,128)(2,1)}), bf16[16,16,1024]{2,1,0:T(8,128)(2,1)S(1)}, u32[]{:S(2)}, u32[]{:S(2)}) %all-to-all-start.1) | async-done | bytes 524320 | tf_op jit(solution)/shard_map/all_to_all | solution.py:88
  33.4 0.9 copy.42
  34.3 66.6 %all-gather.5.cloned.1.call-done = bf16[1,4096,128]{2,1,0:T(8,128)(2,1)} async-done(((bf16[1,128,128]{2,1,0:T(8,128)(2,1)}), bf16[1,4096,128]{2,1,0:T(8,128)(2,1)}) %all-gather.5.cloned.1.call-update) | async-done | bytes 1048592 | tf_op jit(solution)/shard_map/all_gather | solution.py:117
  100.9 13.9 %while.61 = (s32[]{:T(128)}, f32[128,8]{1,0:T(8,128)S(1)}, f32[128,8]{1,0:T(8,128)S(1)}, s32[128]{0:T(128)S(1)}, s32[1,128]{1,0:T(1,128)S(1)}, /*index=5*/bf16[4...) while((s32[]{:T(128)}, f32[128,8]{1,0:T(8,128)S(1)}, ...), condition=%wide.region_6.7_spmd.clone, body=%wide.region_0.6_spmd.clone.sunk | while | flops 137039104 | bytes 6900005 | solution.py:25
  100.9 0.7 and_reduce_fusion.6
  102.2 3.1 conditional.9
  103.3 1.4 fusion.61
  105.4 0.7 and_reduce_fusion.6
  106.7 0.7 and_reduce_fusion.6
  108.1 0.7 and_reduce_fusion.6
  109.4 0.7 and_reduce_fusion.6
  110.8 0.7 and_reduce_fusion.6
  112.1 0.7 and_reduce_fusion.6
  113.5 0.7 and_reduce_fusion.6
  114.8 69.6 %all-gather.7.cloned.1.call-done = bf16[1,4096,128]{2,1,0:T(8,128)(2,1)} async-done(((bf16[1,128,128]{2,1,0:T(8,128)(2,1)}), bf16[1,4096,128]{2,1,0:T(8,128)(2,1)}) %all-gather.7.cloned.1.call-update) | async-done | bytes 1048592 | tf_op jit(solution)/shard_map/all_gather | solution.py:118
  184.4 14.0 %while.62 = (s32[]{:T(128)}, f32[1024,128]{1,0:T(8,128)S(1)}, s32[128]{0:T(128)S(1)}, s32[1,128]{1,0:T(1,128)S(1)}, bf16[4096,128]{1,0:T(8,128)(2,1)}, /*index=5...) while((s32[]{:T(128)}, f32[1024,128]{1,0:T(8,128)S(1)}, ...), condition=%wide.region_11.12_spmd.clone, body=%wide.region_7.11_spmd.clone.sunk | while | flops 271385856 | bytes 3833121 | solution.py:25
  184.5 0.6 and_reduce_fusion.7
  185.8 3.3 conditional.10
  187.0 2.1 fusion.13
  189.1 0.6 and_reduce_fusion.7
  190.4 0.6 and_reduce_fusion.7
  191.8 0.6 and_reduce_fusion.7
  193.1 0.6 and_reduce_fusion.7
  198.5 1.5 fusion.38
  200.2 23.3 %while.63 = (s32[]{:T(128)}, f32[1024,128]{1,0:T(8,128)S(1)}, bf16[4096,256]{0,1:T(8,128)(2,1)S(1)}, s32[128]{0:T(128)S(1)}, s32[1,128]{1,0:T(1,128)S(1)}, /*ind...) while((s32[]{:T(128)}, f32[1024,128]{1,0:T(8,128)S(1)}, ...), condition=%wide.region_17.18_spmd.clone, body=%wide.region_13.17_spmd.clone.sunk | while | flops 676660480 | bytes 14985601 | solution.py:25
  200.2 0.6 and_reduce_fusion.8
  202.0 8.8 %conditional.11 = ((f32[1024,128]{1,0:T(8,128)S(1)}, bf16[4096,256]{0,1:T(8,128)(2,1)S(1)})) conditional(s32[]{:T(128)} %convert_element_type.132, (f32[1024,128]{1,0:T(8,128)S(1)}, bf16[4096,256]{0,1:T(8,128)(2,1)S(1)}) %tuple.222, (s32[]{:T(128)}, s32[1,128]{1,0:T(1,128)S(1)}, s32[128]{0:T(128)}, bf16[4096,128]{1,0:T(8,128)(2,1)}, ...), branch_computations={%region_15.15_spmd, %region_16.16_spmd} | conditional | flops 676659712 | bytes 14984270 | solution.py:73
  202.1 0.7 div.25
  202.8 0.9 sub.89
  203.7 0.7 compare_and_fusion.2
  205.3 1.6 fusion.29
  207.0 1.4 fusion.26
  208.8 1.4 convolution_add_fusion
  210.8 0.6 and_reduce_fusion.8
  223.5 2.5 copy.41
  226.0 0.9 copy-done.2
  227.5 1.1 copy.33
  228.6 6.6 %all-to-all-start = ((bf16[16,16,1024]{2,1,0:T(8,128)(2,1)}), bf16[16,16,1024]{2,1,0:T(8,128)(2,1)S(1)}, u32[]{:S(2)}, u32[]{:S(2)}) async-start(bf16[16,16,1024]{2,1,0:T(8,128)(2,1)} %copy.33), calls=%async_computation | async-start | bytes 1048576 | tf_op jit(solution)/shard_map/all_to_all | solution.py:123
  235.2 0.8 broadcast_in_dim_reshape.8
  236.0 12.8 %all-to-all-done = bf16[16,16,1024]{2,1,0:T(8,128)(2,1)S(1)} async-done(((bf16[16,16,1024]{2,1,0:T(8,128)(2,1)}), bf16[16,16,1024]{2,1,0:T(8,128)(2,1)S(1)}, u32[]{:S(2)}, u32[]{:S(2)}) %all-to-all-start) | async-done | bytes 524320 | tf_op jit(solution)/shard_map/all_to_all | solution.py:123
  249.3 0.9 copy.35
  250.1 167.6 %reduce-scatter.2.cloned.1.call-done = bf16[128,256]{1,0:T(8,128)(2,1)} async-done(((bf16[4096,256]{1,0:T(8,128)(2,1)}), bf16[128,256]{1,0:T(8,128)(2,1)}) %reduce-scatter.2.cloned.1.call-update) | async-done | bytes 65552 | tf_op jit(solution)/shard_map/reduce_scatter | solution.py:174
  417.7 1.4 slice_bitcast_fusion
  (113 shorter events, 18.3 us)
Async XLA Ops:
  7.2 2.0 copy-start
  7.2 13.1 %copy-start.5 = (s32[1,8]{1,0:T(1,128)S(1)}, s32[1,8]{1,0:T(1,128)}, u32[]{:S(2)}) copy-start(s32[1,8]{1,0:T(1,128)} %param.22) | copy-start | bytes 100
  7.2 13.0 %copy-start.4 = (bf16[1,128,1024]{2,1,0:T(8,128)(2,1)S(1)}, bf16[1,128,1024]{2,1,0:T(8,128)(2,1)}, u32[]{:S(2)}) copy-start(bf16[1,128,1024]{2,1,0:T(8,128)(2,1)} %param.18) | copy-start | bytes 786436
  7.2 93.7 %all-gather.5.cloned.1.call-start = ((), (), s32[]{:S(2)}) async-start(), calls=%async_computation.4 | async-start | bytes 1081344 | tf_op jit(solution)/shard_map/all_gather | solution.py:117
  10.7 21.9 %all-to-all-start.1 = ((bf16[16,16,1024]{2,1,0:T(8,128)(2,1)}), bf16[16,16,1024]{2,1,0:T(8,128)(2,1)S(1)}, u32[]{:S(2)}, u32[]{:S(2)}) async-start(bf16[16,16,1024]{2,1,0:T(8,128)(2,1)} %copy.37), calls=%async_computation.1 | async-start | bytes 1048576 | tf_op jit(solution)/shard_map/all_to_all | solution.py:88
  19.3 165.0 %all-gather.7.cloned.1.call-start = ((), (), s32[]{:S(2)}) async-start(), calls=%async_computation.5 | async-start | bytes 1081344 | tf_op jit(solution)/shard_map/all_gather | solution.py:118
  20.1 397.6 %reduce-scatter.2.cloned.1.call-start = ((), (), s32[]{:S(2)}) async-start(), calls=%async_computation.3 | async-start | bytes 2162688 | tf_op jit(solution)/shard_map/reduce_scatter | solution.py:174
  20.2 80.7 %copy-start.3 = (s32[1,128]{1,0:T(1,128)S(1)}, s32[1,128]{1,0:T(1,128)}, u32[]{:S(2)}) copy-start(s32[1,128]{1,0:T(1,128)} %param.21) | copy-start | bytes 1540
  184.4 14.0 %copy-start.1 = (f32[16,8,8,128]{3,2,1,0:T(8,128)S(1)}, f32[16,8,8,128]{3,2,1,0:T(8,128)}, u32[]{:S(2)}) copy-start(f32[16,8,8,128]{3,2,1,0:T(8,128)} %copy.42) | copy-start | bytes 1572868
  226.0 0.9 copy-start.2
  226.0 1.1 copy-start.6
  227.1 21.8 %copy-start.7 = (s32[8]{0:T(128)S(1)}, s32[8]{0:T(128)}, u32[]{:S(2)}) copy-start(s32[8]{0:T(128)} %get-tuple-element.1498) | copy-start | bytes 100
  228.6 20.2 %all-to-all-start = ((bf16[16,16,1024]{2,1,0:T(8,128)(2,1)}), bf16[16,16,1024]{2,1,0:T(8,128)(2,1)S(1)}, u32[]{:S(2)}, u32[]{:S(2)}) async-start(bf16[16,16,1024]{2,1,0:T(8,128)(2,1)} %copy.33), calls=%async_computation | async-start | bytes 1048576 | tf_op jit(solution)/shard_map/all_to_all | solution.py:123
Sparse Core Ops, SparseCore 0:
  11.4 89.4 all-gather.4
  104.2 80.1 all-gather.6
  226.1 191.5 reduce-scatter.1
where the time goes:
time: 432 us; the launch traced here: 426 us
  waiting for transfers between devices  330 us (76%)
  other arithmetic  24.3 us (6%)
  loops' own time  16.6 us (4%)
  starting transfers between devices  15.4 us (4%)
  local copies, waits for them, and re-layouts  15.3 us (4%)
  between operations  14 us (3%)
  matrix products  10.5 us (2%)
    reduce_scatter x1, waiting for transfers between devices, per_device(): lax.psum_scatter(pair_buffer.astype(jnp.bfloat16), 'ctx', scatter_dimensi...  168 us
    all_gather x1, waiting for transfers between devices, per_device(): lax.all_gather(value_states[0], 'ctx', axis=0, tiled=True)  69.6 us
    all_gather x1, waiting for transfers between devices, per_device(): lax.all_gather(key_states[0], 'ctx', axis=0, tiled=True)  66.6 us
    another operation x3, loops' own time, over_tiles(): running = lax.fori_loop(0, full_tiles, tile_step, running)  16.1 us
    reduce_or x24, other arithmetic, guarded(): needed = jnp.any((key_first <= positions) & (key_last >= starts))  15.4 us
    all_to_all x1, waiting for transfers between devices, per_device(): lax.all_to_all(to_slots(attn_rows, ahead_ids), 'dp', split_axis=0, concat...  12.8 us
    all_to_all x1, waiting for transfers between devices, per_device(): lax.all_to_all(to_slots(out_grad[0], behind), 'dp', split_axis=0, concat_...  11.7 us
    all_to_all x1, starting transfers between devices, per_device(): lax.all_to_all(to_slots(out_grad[0], behind), 'dp', split_axis=0, concat_...  8.68 us
  transfers between devices with their start and end apart: 5, of which 5 were waited for; matrix products, arithmetic and copies ran while one was open for 4% of the time, Pallas kernels for 0%

commit v1 on v0

v1 whole, which is shorter than its diff:
```python
import functools
import math

import jax
import jax.numpy as jnp
from jax import lax
from jax.experimental import pallas as pl
from jax.experimental.pallas import tpu as pltpu
from jax.sharding import PartitionSpec as P

HDIM = 128
MASKED = -1e30
MESH = pl.DeviceIdType.MESH
VMEM_LIMIT = 56 * 1024 * 1024
CORES = 2
RING = 8


def place():
    ctx = lax.axis_index("ctx")
    group = lax.axis_index("dp")
    chip = ctx // CORES
    return group, ctx, chip // RING, chip % RING, ctx % CORES


def ctx_of(plane, z, core):
    return (plane * RING + z) * CORES + core


def remote(src, dst, send_sem, recv_sem, **axes):
    return pltpu.make_async_remote_copy(
        src_ref=src, dst_ref=dst, send_sem=send_sem, recv_sem=recv_sem,
        device_id=axes, device_id_type=MESH,
    )


def greet(group, plane, z, core, groups):
    barrier = pltpu.get_barrier_semaphore()

    def hello(**axes):
        pl.semaphore_signal(barrier, inc=1, device_id=axes, device_id_type=MESH)

    def dp_peer(s, carry):
        hello(dp=(group + s) % groups)
        return carry

    def z_peer(s, carry):
        hello(ctx=ctx_of(plane, (z + s) % RING, core))
        return carry

    lax.fori_loop(1, groups, dp_peer, 0)
    lax.fori_loop(1, RING, z_peer, 0)
    hello(ctx=ctx_of(1 - plane, z, core))
    hello(ctx=ctx_of(plane, z, 1 - core))
    pl.semaphore_wait(barrier, groups - 1 + RING - 1 + 2)


def slot_of(plan_ref, s, slots):
    found = jnp.int32(0)
    for t in range(slots):
        found = jnp.where(plan_ref[0, t] == s, jnp.int32(t), found)
    return found


def gather_kernel(groups, slots, k_ref, v_ref, grad_ref, plan_ref, kv_ref, home_ref,
                  stage, landed, send_z, send_x, send_s, recv_kv, send_g, recv_g):
    group, ctx, plane, z, core = place()
    greet(group, plane, z, core, groups)
    kv_ref[ctx, :, :HDIM] = k_ref[0]
    kv_ref[ctx, :, HDIM:] = v_ref[0]

    def z_copy(s):
        return remote(kv_ref.at[ctx], kv_ref.at[ctx], send_z.at[s], recv_kv.at[ctx],
                      ctx=ctx_of(plane, (z + s) % RING, core))

    def x_copy(s):
        block = ctx_of(plane, (z + RING - s) % RING, core)
        return remote(kv_ref.at[block], kv_ref.at[block], send_x.at[s], recv_kv.at[block],
                      ctx=ctx_of(1 - plane, z, core))

    def s_copy(owner, s):
        block = ctx_of(owner, (z + RING - s) % RING, core)
        return remote(kv_ref.at[block], kv_ref.at[block], send_s.at[owner * RING + s],
                      recv_kv.at[block], ctx=ctx_of(plane, z, 1 - core))

    def g_copy(s):
        return remote(stage.at[s], landed.at[s], send_g.at[s], recv_g.at[s],
                      dp=(group + groups - s) % groups)

    def arrived(block):
        remote(kv_ref.at[block], kv_ref.at[block], send_z.at[0], recv_kv.at[block],
               ctx=ctx_of(plane, z, 1 - core)).wait_recv()

    def z_start(s, carry):
        @pl.when((plane == 0) | (z + s < RING))
        def _():
            z_copy(s).start()
        return carry

    lax.fori_loop(1, RING, z_start, 0)

    @pl.when(plane == 0)
    def _():
        x_copy(0).start()

    s_copy(plane, 0).start()

    for s in range(groups):
        block = grad_ref[slot_of(plan_ref, s, slots)]
        if s == 0:
            landed[0] = block
        else:
            stage[s] = block

    def g_start(s, carry):
        g_copy(s).start()
        return carry

    lax.fori_loop(1, groups, g_start, 0)

    def z_land(s, carry):
        @pl.when((plane == 0) | (z >= s))
        def _():
            arrived(ctx_of(plane, (z + RING - s) % RING, core))

            @pl.when(plane == 0)
            def _():
                x_copy(s).start()

            s_copy(plane, s).start()
        return carry

    lax.fori_loop(1, RING, z_land, 0)

    @pl.when(plane == 1)
    def _():
        def x_land(s, carry):
            arrived(ctx_of(0, (z + RING - s) % RING, core))
            s_copy(0, s).start()
            return carry

        lax.fori_loop(0, RING, x_land, 0)

    def sib_land(s, carry):
        @pl.when((plane == 0) | (z >= s))
        def _():
            arrived(ctx_of(plane, (z + RING - s) % RING, 1 - core))
        return carry

    lax.fori_loop(0, RING, sib_land, 0)

    @pl.when(plane == 1)
    def _():
        def sib_x(s, carry):
            arrived(ctx_of(0, (z + RING - s) % RING, 1 - core))
            return carry

        lax.fori_loop(0, RING, sib_x, 0)

    def g_land(s, carry):
        g_copy(s).wait_recv()
        return carry

    lax.fori_loop(1, groups, g_land, 0)
    for t in range(slots):
        home_ref[t] = landed[plan_ref[0, t]]

    def g_left(s, carry):
        g_copy(s).wait_send()
        return carry

    lax.fori_loop(1, groups, g_left, 0)

    def z_left(s, carry):
        @pl.when((plane == 0) | (z + s < RING))
        def _():
            z_copy(s).wait_send()
        return carry

    lax.fori_loop(1, RING, z_left, 0)

    def own_left(s, carry):
        @pl.when(plane == 0)
        def _():
            x_copy(s).wait_send()

        @pl.when((plane == 0) | (z >= s))
        def _():
            s_copy(plane, s).wait_send()

        @pl.when(plane == 1)
        def _():
            s_copy(0, s).wait_send()
        return carry

    lax.fori_loop(0, RING, own_left, 0)


def scatter_kernel(groups, slots, attn_ref, part_ref, plan_ref, moved_ref, kg_ref, vg_ref,
                   stage, landed, sib, pair, xbuf, zbuf,
                   send_s, recv_s, send_x, recv_x, send_z, recv_z, send_g, recv_g):
    group, ctx, plane, z, core = place()
    greet(group, plane, z, core, groups)

    def s_copy(owner):
        return remote(part_ref.at[1 - core, owner], sib.at[owner], send_s.at[owner],
                      recv_s.at[owner], ctx=ctx_of(plane, z, 1 - core))

    def x_copy(s):
        spot = (z + s) % RING
        return remote(pair.at[0, spot], xbuf.at[spot], send_x.at[spot], recv_x.at[spot],
                      ctx=ctx_of(1 - plane, z, core))

    def z_copy(s):
        spot = (z + s) % RING
        return remote(pair.at[plane, spot], zbuf.at[z], send_z.at[s], recv_z.at[z],
                      ctx=ctx_of(plane, spot, core))

    def z_arrived(source):
        remote(zbuf.at[source], zbuf.at[source], send_z.at[0], recv_z.at[source],
               ctx=ctx_of(plane, source, core)).wait_recv()

    def g_copy(s):
        return remote(stage.at[s], landed.at[s], send_g.at[s], recv_g.at[s],
                      dp=(group + s) % groups)

    s_copy(0).start()

    @pl.when(plane == 1)
    def _():
        s_copy(1).start()

    for s in range(groups):
        block = attn_ref[slot_of(plan_ref, s, slots)]
        if s == 0:
            landed[0] = block
        else:
            stage[s] = block

    def g_start(s, carry):
        g_copy(s).start()
        return carry

    lax.fori_loop(1, groups, g_start, 0)

    def add(a, b):
        return (a.astype(jnp.float32) + b.astype(jnp.float32)).astype(jnp.bfloat16)

    s_copy(0).wait_recv()

    def pair_zero(s, carry):
        spot = (z + s) % RING
        pair[0, spot] = add(part_ref[core, 0, spot], sib[0, spot])

        @pl.when(plane == 1)
        def _():
            x_copy(s).start()
        return carry

    lax.fori_loop(0, RING, pair_zero, 0)

    @pl.when(plane == 1)
    def _():
        s_copy(1).wait_recv()

        def pair_one(s, carry):
            pair[1, s] = add(part_ref[core, 1, s], sib[1, s])
            return carry

        lax.fori_loop(0, z + 1, pair_one, 0)

        def z_start(s, carry):
            @pl.when(z + s >= RING)
            def _():
                z_copy(s).start()
            return carry

        lax.fori_loop(1, RING, z_start, 0)

    @pl.when(plane == 0)
    def _():
        def fold(s, carry):
            spot = (z + s) % RING
            x_copy(s).wait_recv()
            pair[0, spot] = add(pair[0, spot], xbuf[spot])

            @pl.when(s > 0)
            def _():
                z_copy(s).start()
            return carry

        lax.fori_loop(0, RING, fold, 0)

    kg_ref[...] = pair[plane, z].astype(jnp.float32)[None]

    def z_land(s, carry):
        @pl.when((plane == 0) | (z + s < RING))
        def _():
            source = (z + s) % RING
            z_arrived(source)
            kg_ref[...] += zbuf[source].astype(jnp.float32)[None]
        return carry

    lax.fori_loop(1, RING, z_land, 0)
    vg_ref[...] = kg_ref[...].astype(jnp.bfloat16)

    def g_land(s, carry):
        g_copy(s).wait_recv()
        return carry

    lax.fori_loop(1, groups, g_land, 0)
    for t in range(slots):
        moved_ref[t] = landed[plan_ref[0, t]]

    def g_left(s, carry):
        g_copy(s).wait_send()
        return carry

    lax.fori_loop(1, groups, g_left, 0)
    s_copy(0).wait_send()

    @pl.when(plane == 1)
    def _():
        s_copy(1).wait_send()

        def x_left(s, carry):
            x_copy(s).wait_send()
            return carry

        lax.fori_loop(0, RING, x_left, 0)

    def z_left(s, carry):
        @pl.when((plane == 0) | (z + s >= RING))
        def _():
            z_copy(s).wait_send()
        return carry

    lax.fori_loop(1, RING, z_left, 0)


NT = (((1,), (1,)), ((), ()))
TN = (((0,), (0,)), ((), ()))
NN = (((1,), (0,)), ((), ()))


def dot(a, b, dims):
    return lax.dot_general(a, b, dims, preferred_element_type=jnp.float32)


def attend_kernel(heads, tile, where_ref, q_ref, g_ref, kv_ref, starts_ref,
                  attn_ref, dq_ref, part_ref,
                  qh, gh, qs, gs, scores, probs, top, total, outT, dqT, dotT):
    tok = q_ref.shape[0]
    rows = heads * tok
    wide = 2 * tok
    scale = 1.0 / math.sqrt(HDIM)
    to_two = scale / math.log(2.0)
    ctx = where_ref[0]
    first = where_ref[1] // tile
    last = ctx * tok // tile
    chunks = [slice(n * wide, (n + 1) * wide) for n in range(rows // wide)]

    for h in range(heads):
        part = slice(h * tok, (h + 1) * tok)
        qh[part] = q_ref[:, h * HDIM:(h + 1) * HDIM]
        gh[part] = g_ref[:, h * HDIM:(h + 1) * HDIM]
    part_ref[...] = jnp.zeros_like(part_ref)
    top[...] = jnp.full_like(top, MASKED)
    total[...] = jnp.zeros_like(total)
    outT[...] = jnp.zeros_like(outT)
    dqT[...] = jnp.zeros_like(dqT)

    def fold(x):
        return x.reshape(tile // 8, 8, x.shape[1])

    def rows_of(n):
        return pl.ds(pl.multiple_of(n * tile, tile), tile)

    def score_tile(n, carry):
        keys = kv_ref[rows_of(n), :HDIM]

        def put(bias):
            for c in chunks:
                s = dot(keys, qh[c], NT)
                if bias is not None:
                    s = s + bias
                scores[n, :, c] = s
                top[:, c] = jnp.maximum(top[:, c], jnp.max(fold(s), axis=0))

        masked = (n * tile < where_ref[2]) | (n == last)

        @pl.when(masked)
        def _():
            at = n * tile + lax.broadcasted_iota(jnp.int32, (tile, tok), 0)
            mine = ctx * tok + lax.broadcasted_iota(jnp.int32, (tile, tok), 1)
            bias = jnp.where((at >= starts_ref[...]) & (at <= mine), 0.0, MASKED)
            put(jnp.concatenate([bias, bias], axis=1))

        @pl.when(jnp.logical_not(masked))
        def _():
            put(None)

        return carry

    lax.fori_loop(first, last + 1, score_tile, 0)
    top[...] = jnp.broadcast_to(jnp.max(top[...], axis=0, keepdims=True) * to_two, top.shape)

    def weigh_tile(n, carry):
        values = kv_ref[rows_of(n), HDIM:]
        for c in chunks:
            p = jnp.exp2(scores[n, :, c] * to_two - top[0:1, c])
            total[:, c] += jnp.sum(fold(p), axis=0)
            p = p.astype(jnp.bfloat16)
            probs[n, :, c] = p
            outT[:, c] += dot(values, p, TN)
        return carry

    lax.fori_loop(first, last + 1, weigh_tile, 0)
    inverse = 1.0 / jnp.sum(total[...], axis=0, keepdims=True)
    total[...] = jnp.broadcast_to(inverse, total.shape)

    ones = jnp.ones((8, HDIM), jnp.bfloat16)
    for h in range(heads):
        part = slice(h * tok, (h + 1) * tok)
        cols = slice(h * HDIM, (h + 1) * HDIM)
        out = (outT[:, part] * total[0:1, part]).T.astype(jnp.bfloat16)
        attn_ref[:, cols] = out
        grad = gh[part].astype(jnp.float32)
        prod = grad * out.astype(jnp.float32)
        high = prod.astype(jnp.bfloat16)
        low = (prod - high.astype(jnp.float32)).astype(jnp.bfloat16)
        dotT[:, part] = dot(ones, high, NT) + dot(ones, low, NT)
        back = jnp.broadcast_to(total[0:1, part], (tok, tok)).T
        gs[part] = (grad * back).astype(jnp.bfloat16)
        qs[part] = (qh[part].astype(jnp.float32) * (back * scale)).astype(jnp.bfloat16)

    def back_tile(n, carry):
        keys = kv_ref[rows_of(n), :HDIM]
        values = kv_ref[rows_of(n), HDIM:]
        dk = jnp.zeros((tile, HDIM), jnp.float32)
        dv = jnp.zeros((tile, HDIM), jnp.float32)
        for c in chunks:
            dp = dot(values, gh[c], NT)
            p = probs[n, :, c]
            ds = (p.astype(jnp.float32) * (dp - dotT[0:1, c])).astype(jnp.bfloat16)
            dqT[:, c] += dot(keys, ds, TN)
            dk += dot(ds, qs[c], NN)
            dv += dot(p, gs[c], NN)
        dk = dk.astype(jnp.bfloat16)
        dv = dv.astype(jnp.bfloat16)
        for core in range(CORES):
            here = slice(core * tok, (core + 1) * tok)
            part_ref[core, n, :, :HDIM] = dk[here]
            part_ref[core, n, :, HDIM:] = dv[here]
        return carry

    lax.fori_loop(first, last + 1, back_tile, 0)
    for h in range(heads):
        part = slice(h * tok, (h + 1) * tok)
        cols = slice(h * HDIM, (h + 1) * HDIM)
        dq_ref[:, cols] = (dqT[:, part] * (total[0:1, part] * scale)).T.astype(jnp.bfloat16)


def attend(where, queries, grads, kv, starts, interpret=False):
    tok, width = queries.shape
    heads = width // HDIM
    rows = heads * tok
    tile = CORES * tok
    tiles = kv.shape[0] // tile
    vmem = pl.BlockSpec(memory_space=pltpu.VMEM)
    bf, f32 = jnp.bfloat16, jnp.float32
    return pl.pallas_call(
        functools.partial(attend_kernel, heads, tile),
        out_shape=(
            jax.ShapeDtypeStruct((tok, width), bf),
            jax.ShapeDtypeStruct((tok, width), bf),
            jax.ShapeDtypeStruct((CORES, tiles, tok, 2 * HDIM), bf),
        ),
        in_specs=[pl.BlockSpec(memory_space=pltpu.SMEM)] + [vmem] * 4,
        out_specs=(vmem,) * 3,
        scratch_shapes=[
            pltpu.VMEM((rows, HDIM), bf),
            pltpu.VMEM((rows, HDIM), bf),
            pltpu.VMEM((rows, HDIM), bf),
            pltpu.VMEM((rows, HDIM), bf),
            pltpu.VMEM((tiles, tile, rows), f32),
            pltpu.VMEM((tiles, tile, rows), bf),
            pltpu.VMEM((8, rows), f32),
            pltpu.VMEM((8, rows), f32),
            pltpu.VMEM((HDIM, rows), f32),
            pltpu.VMEM((HDIM, rows), f32),
            pltpu.VMEM((8, rows), f32),
        ],
        compiler_params=pltpu.CompilerParams(vmem_limit_bytes=VMEM_LIMIT),
        interpret=interpret,
    )(where, queries, grads, kv, starts)


def per_device(queries, key_states, value_states, doc_start, move_plan, out_grad):
    tok, width = queries.shape[1:]
    groups = lax.axis_size("dp")
    pieces = lax.axis_size("ctx")
    slots = move_plan.shape[1]
    rows = tok // slots
    ctx = lax.axis_index("ctx")
    vmem = pl.BlockSpec(memory_space=pltpu.VMEM)
    smem = pl.BlockSpec(memory_space=pltpu.SMEM)
    bf, f32 = jnp.bfloat16, jnp.float32
    dma = pltpu.SemaphoreType.DMA

    kv, home = pl.pallas_call(
        functools.partial(gather_kernel, groups, slots),
        out_shape=(
            jax.ShapeDtypeStruct((pieces, tok, 2 * HDIM), bf),
            jax.ShapeDtypeStruct((slots, rows, width), bf),
        ),
        in_specs=[vmem, vmem, vmem, smem],
        out_specs=(vmem, vmem),
        scratch_shapes=[
            pltpu.VMEM((groups, rows, width), bf),
            pltpu.VMEM((groups, rows, width), bf),
            dma((RING,)), dma((RING,)), dma((2 * RING,)), dma((pieces,)),
            dma((groups,)), dma((groups,)),
        ],
        compiler_params=pltpu.CompilerParams(
            collective_id=0, has_side_effects=True, vmem_limit_bytes=VMEM_LIMIT),
    )(key_states, value_states, out_grad.reshape(slots, rows, width), move_plan)

    where = jnp.stack([ctx, doc_start[0, 0], doc_start[0, tok - 1]]).astype(jnp.int32)
    attn, dq, parts = attend(
        where, queries[0], home.reshape(tok, width), kv.reshape(pieces * tok, 2 * HDIM), doc_start)

    moved, _, pair_grad = pl.pallas_call(
        functools.partial(scatter_kernel, groups, slots),
        out_shape=(
            jax.ShapeDtypeStruct((slots, rows, width), bf),
            jax.ShapeDtypeStruct((1, tok, 2 * HDIM), f32),
            jax.ShapeDtypeStruct((1, tok, 2 * HDIM), bf),
        ),
        in_specs=[vmem, vmem, smem],
        out_specs=(vmem, vmem, vmem),
        scratch_shapes=[
            pltpu.VMEM((groups, rows, width), bf),
            pltpu.VMEM((groups, rows, width), bf),
            pltpu.VMEM((2, RING, tok, 2 * HDIM), bf),
            pltpu.VMEM((2, RING, tok, 2 * HDIM), bf),
            pltpu.VMEM((RING, tok, 2 * HDIM), bf),
            pltpu.VMEM((RING, tok, 2 * HDIM), bf),
            dma((2,)), dma((2,)), dma((RING,)), dma((RING,)), dma((RING,)), dma((RING,)),
            dma((groups,)), dma((groups,)),
        ],
        compiler_params=pltpu.CompilerParams(
            collective_id=1, has_side_effects=True, vmem_limit_bytes=VMEM_LIMIT),
    )(attn.reshape(slots, rows, width), parts.reshape(CORES, 2, RING, tok, 2 * HDIM), move_plan)
    return (
        moved.reshape(1, tok, width),
        dq[None],
        pair_grad[:, :, :HDIM],
        pair_grad[:, :, HDIM:],
    )


def solution(mesh):
    split = P("dp", "ctx", None)
    return jax.shard_map(
        per_device,
        mesh=mesh,
        in_specs=(split, split, split, P("dp", "ctx"), P("ctx", None), split),
        out_specs=(split, split, split, split),
        check_vma=False,
    )
```

time: 432 us -> 113 us (0.26); the launches traced: 426 us -> 113 us
  waiting for transfers between devices: 330 us -> 0 us
  Pallas kernels: 0 us -> 106 us
  other arithmetic: 24.3 us -> 1.94 us
  loops' own time: 16.6 us -> 0 us
  starting transfers between devices: 15.4 us -> 0 us
  between operations: 14 us -> 0.65 us
  local copies, waits for them, and re-layouts: 15.3 us -> 4.39 us
  matrix products: 10.5 us -> 0 us
    reduce_scatter x1 -> x0, waiting for transfers between devices: 168 us -> none  [per_device(): lax.psum_scatter(pair_buffer.astype(jnp.bfloat16), 'ctx', scatter_dimensi...]
    all_gather x2 -> x0, waiting for transfers between devices: 136 us -> none  [the longest x1 69.6 us: per_device(): lax.all_gather(value_states[0], 'ctx', axis=0, tiled=True)]
    pallas_call x0 -> x3, Pallas kernels: none -> 106 us  [the longest x1 63.8 us: per_device(): pl.pallas_call(functools.partial(scatter_kernel, groups, slots), out_shap...]
    all_to_all x2 -> x0, waiting for transfers between devices: 24.5 us -> none  [the longest x1 12.8 us: per_device(): lax.all_to_all(to_slots(attn_rows, ahead_ids), 'dp', split_axis=0, concat...]
    another operation x27 -> x0, loops' own time: 16.6 us -> none  [the longest x3 16.1 us: over_tiles(): running = lax.fori_loop(0, full_tiles, tile_step, running)]
    reduce_or x24 -> x0, other arithmetic: 15.4 us -> none  [guarded(): needed = jnp.any((key_first <= positions) & (key_last >= starts))]
    all_to_all x2 -> x0, starting transfers between devices: 15.2 us -> none  [the longest x1 8.68 us: per_device(): lax.all_to_all(to_slots(out_grad[0], behind), 'dp', split_axis=0, concat_...]
    dot_general x11 -> x0, matrix products: 10.5 us -> none  [the longest x2 3.04 us: scores(): jnp.einsum('rd,nd->rn', query_rows, key_tile, preferred_element_type=jnp....]
  transfers between devices with their start and end apart: 5 -> 0, of which waited for: 5 -> 0; matrix products, arithmetic and copies ran while one was open for 4% -> 0% of each run, Pallas kernels for 0% -> 0%
where the time goes in v1:
time: 113 us
  Pallas kernels  106 us (94%)
  local copies, waits for them, and re-layouts  4.39 us (4%)
  other arithmetic  1.94 us (2%)
    pallas_call x1, Pallas kernels, per_device(): pl.pallas_call(functools.partial(scatter_kernel, groups, slots), out_shap...  63.8 us
    pallas_call x1, Pallas kernels, per_device(): pl.pallas_call(functools.partial(gather_kernel, groups, slots), out_shape...  35.9 us
    pallas_call x1, Pallas kernels, attend(): pl.pallas_call(functools.partial(attend_kernel, heads, tile), out_shape=(...  6.12 us

profile of v1, /device:TPU:1, one launch (start us, length us, event | category | flops | bytes accessed | tf_op | source)
XLA Modules:
  0.0 112.7 jit_solution(9140392000563892312)
XLA Ops:
  0.6 1.3 %fusion.1 = (s32[1,1]{1,0:T(1,128)}, s32[1,1]{1,0:T(1,128)}) fusion(s32[1,128]{1,0:T(1,128)} %starts_ref.1), kind=kLoop, calls=%fused_computation.2 | loop fusion | bytes 16 | tf_op jit(solution)/shard_map/slice | solution.py:529
  1.9 1.9 %pad_add_fusion.where_ref = s32[3]{0:T(128)} fusion(s32[1]{0:T(128)} %bitcast.2, s32[1]{0:T(128)} %bitcast.1, s32[1]{0:T(128)} %bitcast), kind=kLoop, calls=%fused_computation | loop fusion | flops 6 | bytes 24 | tf_op jit(solution)/shard_map/stack | solution.py:529
  3.9 35.9 %shard_map.93 = (bf16[32,128,256]{2,1,0:T(8,128)(2,1)}, bf16[8,16,1024]{2,1,0:T(8,128)(2,1)}) custom-call(bf16[1,128,128]{2,1,0:T(8,128)(2,1)} %k_ref.1, bf16[1,128,128]{2,1,0:T(8,128)(2,1)} %v_ref.1, bf16[8,16,1024]{2,1,0:T(8,128)(2,1)} %bitcast.16, s32[1,8]{1,0:T(1,128)} %plan_ref.3), custom_call_target="tpu_custom_call" | custom-call | tf_op jit(solution)/shard_map/pallas_call | solution.py:511
  39.8 6.1 %shard_map.94 = (bf16[128,1024]{1,0:T(8,128)(2,1)}, bf16[128,1024]{1,0:T(8,128)(2,1)}, bf16[2,16,128,256]{3,2,1,0:T(8,128)(2,1)}) custom-call(s32[3]{0:T(128)} %pad_add_fusion.where_ref, bf16[128,1024]{1,0:T(8,128)(2,1)} %bitcast.13, bf16[128,1024]{1,0:T(8,128)(2,1)} %bitcast.15, bf16[4096,256]{1,0:T(8,128)(2,1)} %bitcast.12, s32[1,128]{1,0:T(1,128)} %starts_ref.1), custom_call_target="tpu_custom_call" | custom-call | tf_op jit(solution)/shard_map/pallas_call | solution.py:472
  45.9 63.8 %shard_map.95 = (bf16[8,16,1024]{2,1,0:T(8,128)(2,1)}, f32[1,128,256]{2,1,0:T(8,128)}, bf16[1,128,256]{2,1,0:T(8,128)(2,1)}) custom-call(bf16[8,16,1024]{2,1,0:T(8,128)(2,1)} %bitcast.14, bf16[2,2,8,128,256]{4,3,2,1,0:T(8,128)(2,1)} %bitcast.11, s32[1,8]{1,0:T(1,128)} %plan_ref.3), custom_call_target="tpu_custom_call" | custom-call | tf_op jit(solution)/shard_map/pallas_call | solution.py:533
  109.7 1.4 %fusion = (bf16[1,128,128]{2,1,0:T(8,128)(2,1)}, bf16[1,128,128]{2,1,0:T(8,128)(2,1)}) fusion(bf16[1,128,256]{2,1,0:T(8,128)(2,1)} %get-tuple-element.17), kind=kLoop, calls=%fused_computation.1 | loop fusion | bytes 131072 | tf_op jit(solution)/shard_map/slice | solution.py:559
  111.1 1.7 %copy.11 = bf16[1,128,1024]{2,1,0:T(8,128)(2,1)} copy(bf16[1,128,1024]{2,1,0:T(8,128)(2,1)} %bitcast.17) | data formatting | bytes 524288

commit v2 on v0

v2 whole, which is shorter than its diff:
```python
import functools
import math

import jax
import jax.numpy as jnp
from jax import lax
from jax.experimental import pallas as pl
from jax.experimental.pallas import tpu as pltpu
from jax.sharding import PartitionSpec as P

HDIM = 128
MASKED = -1e30
MESH = pl.DeviceIdType.MESH
VMEM_LIMIT = 58 * 1024 * 1024
CORES = 2
RING = 8
PAIRS = 8
NT = (((1,), (1,)), ((), ()))
TN = (((0,), (0,)), ((), ()))
NN = (((1,), (0,)), ((), ()))


def dot(a, b, dims):
    return lax.dot_general(a, b, dims, preferred_element_type=jnp.float32)


def add(a, b):
    return (a.astype(jnp.float32) + b.astype(jnp.float32)).astype(jnp.bfloat16)


def ctx_of(plane, z, core):
    return (plane * RING + z) * CORES + core


def remote(src, dst, send_sem, recv_sem, **axes):
    return pltpu.make_async_remote_copy(
        src_ref=src, dst_ref=dst, send_sem=send_sem, recv_sem=recv_sem,
        device_id=axes, device_id_type=MESH,
    )


def loop(low, high, step):
    def body(i, carry):
        step(i)
        return carry

    lax.fori_loop(low, high, body, 0)


def slot_of(plan_ref, s, slots):
    found = jnp.int32(0)
    for t in range(slots):
        found = jnp.where(plan_ref[0, t] == s, jnp.int32(t), found)
    return found


def kernel(groups, slots, heads,
           q_ref, k_ref, v_ref, starts_ref, plan_ref, grad_ref,
           moved_ref, dq_ref, kg_ref, vg_ref,
           kv, qh, gh, qs, gs, scores, probs, top, total, outT, dqT, dotT, attn,
           stage_g, landed_g, stage_o, landed_o, part, sib, pair, xbuf, zbuf, acc,
           send_f, send_x, send_s, recv_kv, send_g, recv_g, send_o, recv_o,
           send_s2, recv_s2, send_x2, recv_x2, send_z2, recv_z2):
    tok = q_ref.shape[0]
    block_rows = tok // slots
    rows = heads * tok
    tile = CORES * tok
    scale = 1.0 / math.sqrt(HDIM)
    to_two = scale / math.log(2.0)
    group = lax.axis_index("dp")
    ctx = lax.axis_index("ctx")
    chip = ctx // CORES
    plane, z, core = chip // RING, chip % RING, ctx % CORES
    own_pair = chip // 2
    wide = rows // 2
    chunks = [slice(n * wide, (n + 1) * wide) for n in range(2)]

    barrier = pltpu.get_barrier_semaphore()

    def hello(**axes):
        pl.semaphore_signal(barrier, inc=1, device_id=axes, device_id_type=MESH)

    loop(1, groups, lambda s: hello(dp=(group + s) % groups))
    loop(1, RING, lambda s: hello(ctx=ctx_of(plane, (z + s) % RING, core)))
    hello(ctx=ctx_of(1 - plane, z, core))
    hello(ctx=ctx_of(plane, z, 1 - core))

    kv[ctx, :, :HDIM] = k_ref[0]
    kv[ctx, :, HDIM:] = v_ref[0]
    for s in range(groups):
        block = grad_ref[slot_of(plan_ref, s, slots)]
        if s == 0:
            landed_g[0] = block
        else:
            stage_g[s] = block
    for h in range(heads):
        qh[h * tok:(h + 1) * tok] = q_ref[:, h * HDIM:(h + 1) * HDIM]
    top[...] = jnp.full_like(top, MASKED)
    total[...] = jnp.zeros_like(total)
    outT[...] = jnp.zeros_like(outT)
    dqT[...] = jnp.zeros_like(dqT)
    pl.semaphore_wait(barrier, groups - 1 + RING - 1 + 2)

    def origin(i):
        hop = (i + 1) // 2
        return (z + jnp.where(i % 2 == 1, RING - hop, hop)) % RING

    def ring_copy(block, sem, ahead):
        return remote(kv.at[block], kv.at[block], send_f.at[sem], recv_kv.at[block],
                      ctx=ctx_of(plane, (z + jnp.where(ahead, 1, RING - 1)) % RING, core))

    def f_copy(i):
        return ring_copy(ctx_of(plane, origin(i), core), i, i % 2 == 1)

    def x_copy(i):
        block = ctx_of(0, origin(i), core)
        return remote(kv.at[block], kv.at[block], send_x.at[i], recv_kv.at[block],
                      ctx=ctx_of(1, z, core))

    def s_copy(owner, i):
        block = ctx_of(owner, origin(i), core)
        return remote(kv.at[block], kv.at[block], send_s.at[owner * RING + i],
                      recv_kv.at[block], ctx=ctx_of(plane, z, 1 - core))

    def g_copy(s):
        return remote(stage_g.at[s], landed_g.at[s], send_g.at[s], recv_g.at[s],
                      dp=(group + groups - s) % groups)

    def o_copy(s):
        return remote(stage_o.at[s], landed_o.at[s], send_o.at[s], recv_o.at[s],
                      dp=(group + s) % groups)

    def arrived(block):
        remote(kv.at[block], kv.at[block], send_f.at[0], recv_kv.at[block],
               ctx=ctx_of(plane, z, 1 - core)).wait_recv()

    ring_copy(ctx, 0, True).start()
    ring_copy(ctx, 6, False).start()

    @pl.when(plane == 0)
    def _():
        x_copy(0).start()

    s_copy(plane, 0).start()
    loop(1, groups, lambda s: g_copy(s).start())

    def fold(x):
        return x.reshape(x.shape[0] // 8, 8, x.shape[1])

    def score(n):
        keys = kv[pl.ds(CORES * n, CORES), :, :HDIM].reshape(tile, HDIM)
        at = n * tile + lax.broadcasted_iota(jnp.int32, (tile, tok), 0)
        mine = ctx * tok + lax.broadcasted_iota(jnp.int32, (tile, tok), 1)
        bias = jnp.where((at >= starts_ref[...]) & (at <= mine), 0.0, MASKED)
        bias = jnp.concatenate([bias] * (wide // tok), axis=1)
        for c in chunks:
            s = dot(keys, qh[c], NT) + bias
            scores[n, :, c] = s
            top[:, c] = jnp.maximum(top[:, c], jnp.max(fold(s), axis=0))

    def gather_step(i):
        @pl.when((i >= 1) & (i < RING))
        def _():
            arrived(ctx_of(plane, origin(i), core))

            @pl.when(i < RING - 2)
            def _():
                f_copy(i).start()

            @pl.when(plane == 0)
            def _():
                x_copy(i).start()

            s_copy(plane, i).start()

        @pl.when((plane == 1) & (i >= 1) & (i <= RING))
        def _():
            arrived(ctx_of(0, origin(i - 1), core))
            s_copy(0, i - 1).start()

        @pl.when((i >= 1) & (i <= RING))
        def _():
            near = plane * RING + origin(i - 1)
            arrived(CORES * near + 1 - core)

            @pl.when(near <= 2 * own_pair + 1)
            def _():
                score(near)

        @pl.when((plane == 1) & (i >= 2))
        def _():
            arrived(CORES * origin(i - 2) + 1 - core)
            score(origin(i - 2))

    loop(0, RING + 2, gather_step)
    top[...] = jnp.broadcast_to(jnp.max(top[...], axis=0, keepdims=True) * to_two, top.shape)

    def weigh(u):
        values = kv[pl.ds(2 * CORES * u, 2 * CORES), :, HDIM:].reshape(2 * tile, HDIM)
        for c in chunks:
            s = scores[pl.ds(2 * u, 2), :, c].reshape(2 * tile, wide)
            p = jnp.exp2(s * to_two - top[0:1, c])
            total[:, c] += jnp.sum(fold(p), axis=0)
            p = p.astype(jnp.bfloat16)
            probs[u, :, c] = p
            outT[:, c] += dot(values, p, TN)

    loop(0, own_pair + 1, weigh)
    inverse = 1.0 / jnp.sum(total[...], axis=0, keepdims=True)
    total[...] = jnp.broadcast_to(inverse, total.shape)
    for h in range(heads):
        mine = slice(h * tok, (h + 1) * tok)
        out = (outT[:, mine] * total[0:1, mine]).T.astype(jnp.bfloat16)
        attn[:, :, h * HDIM:(h + 1) * HDIM] = out.reshape(slots, block_rows, HDIM)
    for s in range(groups):
        block = attn[slot_of(plan_ref, s, slots)]
        if s == 0:
            landed_o[0] = block
        else:
            stage_o[s] = block
    loop(1, groups, lambda s: o_copy(s).start())

    loop(1, groups, lambda s: g_copy(s).wait_recv())
    for t in range(slots):
        block = landed_g[plan_ref[0, t]]
        for h in range(heads):
            first = h * tok + t * block_rows
            gh[first:first + block_rows] = block[:, h * HDIM:(h + 1) * HDIM]
    ones = jnp.ones((8, HDIM), jnp.bfloat16)
    for h in range(heads):
        mine = slice(h * tok, (h + 1) * tok)
        out = attn[:, :, h * HDIM:(h + 1) * HDIM].reshape(tok, HDIM)
        grad = gh[mine].astype(jnp.float32)
        prod = grad * out.astype(jnp.float32)
        high = prod.astype(jnp.bfloat16)
        low = (prod - high.astype(jnp.float32)).astype(jnp.bfloat16)
        dotT[:, mine] = dot(ones, high, NT) + dot(ones, low, NT)
        back = jnp.broadcast_to(total[0:1, mine], (tok, tok)).T
        gs[mine] = (grad * back).astype(jnp.bfloat16)
        qs[mine] = (qh[mine].astype(jnp.float32) * (back * scale)).astype(jnp.bfloat16)

    far = plane * (PAIRS // 2)

    def pair_at(i):
        return jnp.where(i < far, (z // 2 + 1 + i) % (PAIRS // 2), far + z // 2 - (i - far))

    def s2_copy(u):
        return remote(part.at[u, 1 - core], sib.at[u], send_s2.at[u], recv_s2.at[u],
                      ctx=ctx_of(plane, z, 1 - core))

    def x2_copy(u):
        return remote(pair.at[u], xbuf.at[u], send_x2.at[u], recv_x2.at[u],
                      ctx=ctx_of(1 - plane, z, core))

    def z2_copy(spot):
        return remote(pair.at[far + spot // 2, spot % 2], zbuf.at[z], send_z2.at[spot],
                      recv_z2.at[z], ctx=ctx_of(plane, spot, core))

    def back(u):
        keys = kv[pl.ds(2 * CORES * u, 2 * CORES), :, :HDIM].reshape(2 * tile, HDIM)
        values = kv[pl.ds(2 * CORES * u, 2 * CORES), :, HDIM:].reshape(2 * tile, HDIM)
        dp = dot(values, gh[...], NT)
        p = probs[u]
        ds = (p.astype(jnp.float32) * (dp - dotT[0:1])).astype(jnp.bfloat16)
        dqT[...] += dot(keys, ds, TN)
        dk = dot(ds, qs[...], NN).astype(jnp.bfloat16)
        dv = dot(p, gs[...], NN).astype(jnp.bfloat16)
        for which in range(2):
            for c in range(CORES):
                first = (which * CORES + c) * tok
                part[u, c, which, :, :HDIM] = dk[first:first + tok]
                part[u, c, which, :, HDIM:] = dv[first:first + tok]

    def pass_on(u):
        s2_copy(u).wait_recv()
        pair[u] = add(part[u, core], sib[u])

        @pl.when(u < far)
        def _():
            x2_copy(u).start()

        @pl.when((plane == 1) & (u >= far))
        def _():
            for which in range(2):
                spot = (u - far) * 2 + which

                @pl.when(spot < z)
                def _():
                    z2_copy(spot).start()

    def back_step(i):
        u = pair_at(i)
        back(u)
        s2_copy(u).start()

        @pl.when(i >= 1)
        def _():
            pass_on(pair_at(i - 1))

    loop(0, own_pair + 1, back_step)
    pass_on(pair_at(own_pair))

    for h in range(heads):
        mine = slice(h * tok, (h + 1) * tok)
        dq_ref[:, h * HDIM:(h + 1) * HDIM] = (
            dqT[:, mine] * (total[0:1, mine] * scale)).T.astype(jnp.bfloat16)

    @pl.when(plane == 0)
    def _():
        def fold_in(j):
            u = (z // 2 + 1 + j) % (PAIRS // 2)
            x2_copy(u).wait_recv()

            @pl.when(u <= own_pair)
            def _():
                pair[u] = add(pair[u], xbuf[u])

            @pl.when(u > own_pair)
            def _():
                pair[u] = xbuf[u]

            for which in range(2):
                spot = u * 2 + which

                @pl.when(spot != z)
                def _():
                    z2_copy(spot).start()

        loop(0, PAIRS // 2, fold_in)

    acc[...] = pair[own_pair, z % 2].astype(jnp.float32)

    def z_land(s):
        source = (z + s) % RING

        @pl.when((plane == 0) | (source > z))
        def _():
            remote(zbuf.at[source], zbuf.at[source], send_z2.at[0], recv_z2.at[source],
                   ctx=ctx_of(plane, source, core)).wait_recv()
            acc[...] += zbuf[source].astype(jnp.float32)

    loop(1, RING, z_land)
    kg_ref[0] = acc[:, :HDIM].astype(jnp.bfloat16)
    vg_ref[0] = acc[:, HDIM:].astype(jnp.bfloat16)

    loop(1, groups, lambda s: o_copy(s).wait_recv())
    for t in range(slots):
        moved_ref[t] = landed_o[plan_ref[0, t]]

    def exchanged(s):
        g_copy(s).wait_send()
        o_copy(s).wait_send()

    loop(1, groups, exchanged)
    ring_copy(ctx, 0, True).wait_send()
    ring_copy(ctx, 6, False).wait_send()
    loop(1, RING - 2, lambda i: f_copy(i).wait_send())

    def gathered(i):
        s_copy(plane, i).wait_send()

        @pl.when(plane == 0)
        def _():
            x_copy(i).wait_send()

        @pl.when(plane == 1)
        def _():
            s_copy(0, i).wait_send()

        @pl.when((i < z) | ((plane == 0) & (i != z)))
        def _():
            z2_copy(i).wait_send()

        @pl.when(i < far)
        def _():
            x2_copy(i).wait_send()

    loop(0, RING, gathered)
    loop(0, own_pair + 1, lambda i: s2_copy(pair_at(i)).wait_send())


def per_device(queries, key_states, value_states, doc_start, move_plan, out_grad):
    tok, width = queries.shape[1:]
    heads = width // HDIM
    rows = heads * tok
    groups = lax.axis_size("dp")
    pieces = lax.axis_size("ctx")
    slots = move_plan.shape[1]
    block_rows = tok // slots
    tile = CORES * tok
    vmem = pl.BlockSpec(memory_space=pltpu.VMEM)
    smem = pl.BlockSpec(memory_space=pltpu.SMEM)
    bf, f32 = jnp.bfloat16, jnp.float32
    dma = pltpu.SemaphoreType.DMA
    blocks = pltpu.VMEM((groups, block_rows, width), bf)
    heads_bf = pltpu.VMEM((rows, HDIM), bf)

    moved, dq, kg, vg = pl.pallas_call(
        functools.partial(kernel, groups, slots, heads),
        out_shape=(
            jax.ShapeDtypeStruct((slots, block_rows, width), bf),
            jax.ShapeDtypeStruct((tok, width), bf),
            jax.ShapeDtypeStruct((1, tok, HDIM), bf),
            jax.ShapeDtypeStruct((1, tok, HDIM), bf),
        ),
        in_specs=[vmem, vmem, vmem, vmem, smem, vmem],
        out_specs=(vmem,) * 4,
        scratch_shapes=[
            pltpu.VMEM((pieces, tok, 2 * HDIM), bf),
            heads_bf, heads_bf, heads_bf, heads_bf,
            pltpu.VMEM((2 * PAIRS, tile, rows), f32),
            pltpu.VMEM((PAIRS, 2 * tile, rows), bf),
            pltpu.VMEM((8, rows), f32),
            pltpu.VMEM((8, rows), f32),
            pltpu.VMEM((HDIM, rows), f32),
            pltpu.VMEM((HDIM, rows), f32),
            pltpu.VMEM((8, rows), f32),
            pltpu.VMEM((slots, block_rows, width), bf),
            blocks, blocks, blocks, blocks,
            pltpu.VMEM((PAIRS, CORES, 2, tok, 2 * HDIM), bf),
            pltpu.VMEM((PAIRS, 2, tok, 2 * HDIM), bf),
            pltpu.VMEM((PAIRS, 2, tok, 2 * HDIM), bf),
            pltpu.VMEM((PAIRS // 2, 2, tok, 2 * HDIM), bf),
            pltpu.VMEM((RING, tok, 2 * HDIM), bf),
            pltpu.VMEM((tok, 2 * HDIM), f32),
            dma((RING,)), dma((RING,)), dma((2 * RING,)), dma((pieces,)),
            dma((groups,)), dma((groups,)), dma((groups,)), dma((groups,)),
            dma((PAIRS,)), dma((PAIRS,)), dma((PAIRS // 2,)), dma((PAIRS // 2,)),
            dma((RING,)), dma((RING,)),
        ],
        compiler_params=pltpu.CompilerParams(
            collective_id=0, has_side_effects=True, vmem_limit_bytes=VMEM_LIMIT),
    )(
        queries[0], key_states, value_states, doc_start, move_plan,
        out_grad.reshape(slots, block_rows, width),
    )
    return moved.reshape(1, tok, width), dq[None], kg, vg


def solution(mesh):
    split = P("dp", "ctx", None)
    return jax.shard_map(
        per_device,
        mesh=mesh,
        in_specs=(split, split, split, P("dp", "ctx"), P("ctx", None), split),
        out_specs=(split, split, split, split),
        check_vma=False,
    )
```

time: 432 us -> 76 us (0.18); the launches traced: 426 us -> 75.7 us
  waiting for transfers between devices: 330 us -> 0 us
  Pallas kernels: 0 us -> 71.1 us
  other arithmetic: 24.3 us -> 0 us
  loops' own time: 16.6 us -> 0 us
  starting transfers between devices: 15.4 us -> 0 us
  between operations: 14 us -> 0.65 us
  local copies, waits for them, and re-layouts: 15.3 us -> 3.86 us
  matrix products: 10.5 us -> 0 us
    reduce_scatter x1 -> x0, waiting for transfers between devices: 168 us -> none  [per_device(): lax.psum_scatter(pair_buffer.astype(jnp.bfloat16), 'ctx', scatter_dimensi...]
    all_gather x2 -> x0, waiting for transfers between devices: 136 us -> none  [the longest x1 69.6 us: per_device(): lax.all_gather(value_states[0], 'ctx', axis=0, tiled=True)]
    pallas_call x0 -> x1, Pallas kernels: none -> 71.1 us  [per_device(): pl.pallas_call(functools.partial(kernel, groups, slots, heads), out_shape...]
    all_to_all x2 -> x0, waiting for transfers between devices: 24.5 us -> none  [the longest x1 12.8 us: per_device(): lax.all_to_all(to_slots(attn_rows, ahead_ids), 'dp', split_axis=0, concat...]
    another operation x27 -> x0, loops' own time: 16.6 us -> none  [the longest x3 16.1 us: over_tiles(): running = lax.fori_loop(0, full_tiles, tile_step, running)]
    reduce_or x24 -> x0, other arithmetic: 15.4 us -> none  [guarded(): needed = jnp.any((key_first <= positions) & (key_last >= starts))]
    all_to_all x2 -> x0, starting transfers between devices: 15.2 us -> none  [the longest x1 8.68 us: per_device(): lax.all_to_all(to_slots(out_grad[0], behind), 'dp', split_axis=0, concat_...]
    dot_general x11 -> x0, matrix products: 10.5 us -> none  [the longest x2 3.04 us: scores(): jnp.einsum('rd,nd->rn', query_rows, key_tile, preferred_element_type=jnp....]
  transfers between devices with their start and end apart: 5 -> 0, of which waited for: 5 -> 0; matrix products, arithmetic and copies ran while one was open for 4% -> 0% of each run, Pallas kernels for 0% -> 0%
where the time goes in v2:
time: 76 us; the launch traced here: 75.7 us
  Pallas kernels  71.1 us (94%)
  local copies, waits for them, and re-layouts  3.86 us (5%)
    pallas_call x1, Pallas kernels, per_device(): pl.pallas_call(functools.partial(kernel, groups, slots, heads), out_shape...  71.1 us
    unnamed x10, local copies, waits for them, and re-layouts  3.86 us

profile of v2, /device:TPU:1, one launch (start us, length us, event | category | flops | bytes accessed | tf_op | source)
XLA Modules:
  0.0 75.7 jit_solution(11496942328808989344)
XLA Ops:
  0.6 71.1 %shard_map.93 = (bf16[8,16,1024]{2,1,0:T(8,128)(2,1)}, bf16[128,1024]{1,0:T(8,128)(2,1)}, bf16[1,128,128]{2,1,0:T(8,128)(2,1)}, bf16[1,128,128]{2,1,0:T(8,128)(2,1)}) custom-call(bf16[128,1024]{1,0:T(8,128)(2,1)} %bitcast.4, bf16[1,128,128]{2,1,0:T(8,128)(2,1)} %k_ref.1, bf16[1,128,128]{2,1,0:T(8,128)(2,1)} %v_ref.1, s32[1,128]{1,0:T(1,128)} %starts_ref.1, ...), custom_call_target="tpu_custom_call" | custom-call | tf_op jit(solution)/shard_map/pallas_call | solution.py:398
  71.8 0.0 copy-start
  71.8 1.7 %copy.14 = bf16[1,128,1024]{2,1,0:T(8,128)(2,1)} copy(bf16[1,128,1024]{2,1,0:T(8,128)(2,1)} %bitcast.7) | data formatting | bytes 524288
  73.5 0.0 copy-done
  73.5 0.0 copy-start.2
  73.5 0.7 copy.15
  74.2 0.1 copy-done.2
  74.3 0.0 copy-start.1
  74.3 0.6 copy.16
  74.9 0.2 copy-done.1
  75.0 0.6 copy.17
Async XLA Ops:
  71.8 1.7 %copy-start = (bf16[128,1024]{1,0:T(8,128)(2,1)S(1)}, bf16[128,1024]{1,0:T(8,128)(2,1)}, u32[]{:S(2)}) copy-start(bf16[128,1024]{1,0:T(8,128)(2,1)} %get-tuple-element.9) | copy-start | bytes 786436
  73.5 0.8 %copy-start.2 = (bf16[1,128,128]{2,1,0:T(8,128)(2,1)S(1)}, bf16[1,128,128]{2,1,0:T(8,128)(2,1)}, u32[]{:S(2)}) copy-start(bf16[1,128,128]{2,1,0:T(8,128)(2,1)} %get-tuple-element.18) | copy-start | bytes 98308
  74.3 0.8 %copy-start.1 = (bf16[1,128,128]{2,1,0:T(8,128)(2,1)S(1)}, bf16[1,128,128]{2,1,0:T(8,128)(2,1)}, u32[]{:S(2)}) copy-start(bf16[1,128,128]{2,1,0:T(8,128)(2,1)} %get-tuple-element.19) | copy-start | bytes 98308

commit v3 on v2

--- a/solution.py
+++ b/solution.py
@@ -57,7 +57,7 @@
 def kernel(groups, slots, heads,
            q_ref, k_ref, v_ref, starts_ref, plan_ref, grad_ref,
            moved_ref, dq_ref, kg_ref, vg_ref,
-           kv, qh, gh, qs, gs, scores, probs, top, total, outT, dqT, dotT, attn,
+           keys_all, values_all, eye, qh, gh, qs, gs, scores, probs, top, total, outT, dqT, dotT, attn,
            stage_g, landed_g, stage_o, landed_o, part, sib, pair, xbuf, zbuf, acc,
            send_f, send_x, send_s, recv_kv, send_g, recv_g, send_o, recv_o,
            send_s2, recv_s2, send_x2, recv_x2, send_z2, recv_z2):
@@ -75,6 +75,9 @@
     wide = rows // 2
     chunks = [slice(n * wide, (n + 1) * wide) for n in range(2)]
 
+    def flip(x):
+        return dot(eye[...], x, NT)
+
     barrier = pltpu.get_barrier_semaphore()
 
     def hello(**axes):
@@ -85,8 +88,8 @@
     hello(ctx=ctx_of(1 - plane, z, core))
     hello(ctx=ctx_of(plane, z, 1 - core))
 
-    kv[ctx, :, :HDIM] = k_ref[0]
-    kv[ctx, :, HDIM:] = v_ref[0]
+    keys_all[ctx] = k_ref[0]
+    values_all[ctx] = v_ref[0]
     for s in range(groups):
         block = grad_ref[slot_of(plan_ref, s, slots)]
         if s == 0:
@@ -95,32 +98,64 @@
             stage_g[s] = block
     for h in range(heads):
         qh[h * tok:(h + 1) * tok] = q_ref[:, h * HDIM:(h + 1) * HDIM]
+    eye[...] = jnp.where(
+        lax.broadcasted_iota(jnp.int32, (tok, tok), 0)
+        == lax.broadcasted_iota(jnp.int32, (tok, tok), 1), 1.0, 0.0).astype(jnp.bfloat16)
     top[...] = jnp.full_like(top, MASKED)
     total[...] = jnp.zeros_like(total)
     outT[...] = jnp.zeros_like(outT)
     dqT[...] = jnp.zeros_like(dqT)
     pl.semaphore_wait(barrier, groups - 1 + RING - 1 + 2)
 
+    def offset(i):
+        return jnp.where(i == 0, 0, jnp.where(i % 2 == 1, RING // 2 + i // 2, RING // 2 - i // 2))
+
     def origin(i):
+        return (z + RING - offset(i)) % RING
+
+    def goes(i):
+        return (plane == 0) | ((z + offset(i)) % RING >= z // 2 * 2)
+
+    def comes(i):
+        return (plane == 0) | (origin(i) <= z // 2 * 2 + 1)
+
+    def around(i):
         hop = (i + 1) // 2
         return (z + jnp.where(i % 2 == 1, RING - hop, hop)) % RING
 
-    def ring_copy(block, sem, ahead):
-        return remote(kv.at[block], kv.at[block], send_f.at[sem], recv_kv.at[block],
+    def stream(kind):
+        return (keys_all, 0) if kind == 0 else (values_all, 1)
+
+    def source(kind, i):
+        return origin(i) if kind == 0 else around(i)
+
+    def f_copy(i):
+        return remote(keys_all.at[ctx], keys_all.at[ctx], send_f.at[0, i], recv_kv.at[0, ctx],
+                      ctx=ctx_of(plane, (z + offset(i)) % RING, core))
+
+    def ring_copy(kind, i, sem, ahead):
+        block = ctx_of(0 if kind == 2 else plane, around(i), core)
+        return remote(values_all.at[block], values_all.at[block], send_f.at[kind, sem],
+                      recv_kv.at[1, block],
                       ctx=ctx_of(plane, (z + jnp.where(ahead, 1, RING - 1)) % RING, core))
 
-    def f_copy(i):
-        return ring_copy(ctx_of(plane, origin(i), core), i, i % 2 == 1)
-
-    def x_copy(i):
-        block = ctx_of(0, origin(i), core)
-        return remote(kv.at[block], kv.at[block], send_x.at[i], recv_kv.at[block],
+    def r_copy(kind, i):
+        return ring_copy(kind, i, i, i % 2 == 1)
+
+    def first_copy(kind, ahead):
+        return ring_copy(kind, 0, 0 if ahead else RING - 1, ahead)
+
+    def x_copy(kind, i):
+        buf, which = stream(kind)
+        block = ctx_of(0, source(kind, i), core)
+        return remote(buf.at[block], buf.at[block], send_x.at[which, i], recv_kv.at[which, block],
                       ctx=ctx_of(1, z, core))
 
-    def s_copy(owner, i):
-        block = ctx_of(owner, origin(i), core)
-        return remote(kv.at[block], kv.at[block], send_s.at[owner * RING + i],
-                      recv_kv.at[block], ctx=ctx_of(plane, z, 1 - core))
+    def s_copy(kind, owner, i):
+        buf, which = stream(kind)
+        block = ctx_of(owner, source(kind, i), core)
+        return remote(buf.at[block], buf.at[block], send_s.at[which, owner * RING + i],
+                      recv_kv.at[which, block], ctx=ctx_of(plane, z, 1 - core))
 
     def g_copy(s):
         return remote(stage_g.at[s], landed_g.at[s], send_g.at[s], recv_g.at[s],
@@ -130,25 +165,33 @@
         return remote(stage_o.at[s], landed_o.at[s], send_o.at[s], recv_o.at[s],
                       dp=(group + s) % groups)
 
-    def arrived(block):
-        remote(kv.at[block], kv.at[block], send_f.at[0], recv_kv.at[block],
+    def arrived(kind, block):
+        buf, which = stream(kind)
+        remote(buf.at[block], buf.at[block], send_f.at[0, 0], recv_kv.at[which, block],
                ctx=ctx_of(plane, z, 1 - core)).wait_recv()
 
-    ring_copy(ctx, 0, True).start()
-    ring_copy(ctx, 6, False).start()
-
-    @pl.when(plane == 0)
-    def _():
-        x_copy(0).start()
-
-    s_copy(plane, 0).start()
+    for kind in range(2):
+        s_copy(kind, plane, 0).start()
+
+        @pl.when(plane == 0)
+        def _():
+            x_copy(kind, 0).start()
+
+    def spread_out(i):
+        @pl.when(goes(i))
+        def _():
+            f_copy(i).start()
+
+    loop(1, RING, spread_out)
+    first_copy(1, True).start()
+    first_copy(1, False).start()
     loop(1, groups, lambda s: g_copy(s).start())
 
     def fold(x):
         return x.reshape(x.shape[0] // 8, 8, x.shape[1])
 
     def score(n):
-        keys = kv[pl.ds(CORES * n, CORES), :, :HDIM].reshape(tile, HDIM)
+        keys = keys_all[pl.ds(CORES * n, CORES)].reshape(tile, HDIM)
         at = n * tile + lax.broadcasted_iota(jnp.int32, (tile, tok), 0)
         mine = ctx * tok + lax.broadcasted_iota(jnp.int32, (tile, tok), 1)
         bias = jnp.where((at >= starts_ref[...]) & (at <= mine), 0.0, MASKED)
@@ -161,27 +204,49 @@
     def gather_step(i):
         @pl.when((i >= 1) & (i < RING))
         def _():
-            arrived(ctx_of(plane, origin(i), core))
+            @pl.when(comes(i))
+            def _():
+                arrived(0, ctx_of(plane, origin(i), core))
+
+                @pl.when(plane == 0)
+                def _():
+                    x_copy(0, i).start()
+
+                s_copy(0, plane, i).start()
+
+            arrived(1, ctx_of(plane, around(i), core))
 
             @pl.when(i < RING - 2)
             def _():
-                f_copy(i).start()
-
-            @pl.when(plane == 0)
-            def _():
-                x_copy(i).start()
-
-            s_copy(plane, i).start()
+                r_copy(1, i).start()
+
+            s_copy(1, plane, i).start()
 
         @pl.when((plane == 1) & (i >= 1) & (i <= RING))
         def _():
-            arrived(ctx_of(0, origin(i - 1), core))
-            s_copy(0, i - 1).start()
+            j = i - 1
+            arrived(0, ctx_of(0, origin(j), core))
+            s_copy(0, 0, j).start()
+            arrived(1, ctx_of(0, around(j), core))
+
+            @pl.when(j == 0)
+            def _():
+                first_copy(2, True).start()
+                first_copy(2, False).start()
+
+            @pl.when((j >= 1) & (j < RING - 2))
+            def _():
+                r_copy(2, j).start()
+
+            s_copy(1, 0, j).start()
 
         @pl.when((i >= 1) & (i <= RING))
         def _():
             near = plane * RING + origin(i - 1)
-            arrived(CORES * near + 1 - core)
+
+            @pl.when(comes(i - 1))
+            def _():
+                arrived(0, CORES * near + 1 - core)
 
             @pl.when(near <= 2 * own_pair + 1)
             def _():
@@ -189,14 +254,20 @@
 
         @pl.when((plane == 1) & (i >= 2))
         def _():
-            arrived(CORES * origin(i - 2) + 1 - core)
+            arrived(0, CORES * origin(i - 2) + 1 - core)
             score(origin(i - 2))
 
     loop(0, RING + 2, gather_step)
     top[...] = jnp.broadcast_to(jnp.max(top[...], axis=0, keepdims=True) * to_two, top.shape)
 
+    loop(0, RING, lambda i: arrived(1, ctx_of(plane, i, 1 - core)))
+
+    @pl.when(plane == 1)
+    def _():
+        loop(0, RING, lambda i: arrived(1, ctx_of(0, i, 1 - core)))
+
     def weigh(u):
-        values = kv[pl.ds(2 * CORES * u, 2 * CORES), :, HDIM:].reshape(2 * tile, HDIM)
+        values = values_all[pl.ds(2 * CORES * u, 2 * CORES)].reshape(2 * tile, HDIM)
         for c in chunks:
             s = scores[pl.ds(2 * u, 2), :, c].reshape(2 * tile, wide)
             p = jnp.exp2(s * to_two - top[0:1, c])
@@ -210,7 +281,7 @@
     total[...] = jnp.broadcast_to(inverse, total.shape)
     for h in range(heads):
         mine = slice(h * tok, (h + 1) * tok)
-        out = (outT[:, mine] * total[0:1, mine]).T.astype(jnp.bfloat16)
+        out = flip((outT[:, mine] * total[0:1, mine]).astype(jnp.bfloat16)).astype(jnp.bfloat16)
         attn[:, :, h * HDIM:(h + 1) * HDIM] = out.reshape(slots, block_rows, HDIM)
     for s in range(groups):
         block = attn[slot_of(plan_ref, s, slots)]
@@ -235,14 +306,27 @@
         high = prod.astype(jnp.bfloat16)
         low = (prod - high.astype(jnp.float32)).astype(jnp.bfloat16)
         dotT[:, mine] = dot(ones, high, NT) + dot(ones, low, NT)
-        back = jnp.broadcast_to(total[0:1, mine], (tok, tok)).T
+        spread = jnp.broadcast_to(total[0:1, mine], (HDIM, tok))
+        coarse = spread.astype(jnp.bfloat16)
+        fine = (spread - coarse.astype(jnp.float32)).astype(jnp.bfloat16)
+        back = flip(coarse) + flip(fine)
         gs[mine] = (grad * back).astype(jnp.bfloat16)
         qs[mine] = (qh[mine].astype(jnp.float32) * (back * scale)).astype(jnp.bfloat16)
 
     far = plane * (PAIRS // 2)
 
+    near_pairs = z // 2 + 1
+
+    def far_pair(turn):
+        flip_way = (turn == 1) == (z // 2 % 2 == 0)
+        step = jnp.where(turn == 0, 2, jnp.where(turn == 3, 0, jnp.where(flip_way, 1, 3)))
+        return (z // 2 + step) % (PAIRS // 2)
+
     def pair_at(i):
-        return jnp.where(i < far, (z // 2 + 1 + i) % (PAIRS // 2), far + z // 2 - (i - far))
+        away = (plane == 1) & ((i % 2 == 0) | (i >= 2 * near_pairs))
+        turn = jnp.where(i < 2 * near_pairs, i // 2, i - near_pairs)
+        near = (2 * near_pairs - 2 - jnp.where(plane == 1, turn, i)) % near_pairs
+        return jnp.where(away, far_pair(turn), far + near)
 
     def s2_copy(u):
         return remote(part.at[u, 1 - core], sib.at[u], send_s2.at[u], recv_s2.at[u],
@@ -257,8 +341,8 @@
                       recv_z2.at[z], ctx=ctx_of(plane, spot, core))
 
     def back(u):
-        keys = kv[pl.ds(2 * CORES * u, 2 * CORES), :, :HDIM].reshape(2 * tile, HDIM)
-        values = kv[pl.ds(2 * CORES * u, 2 * CORES), :, HDIM:].reshape(2 * tile, HDIM)
+        keys = keys_all[pl.ds(2 * CORES * u, 2 * CORES)].reshape(2 * tile, HDIM)
+        values = values_all[pl.ds(2 * CORES * u, 2 * CORES)].reshape(2 * tile, HDIM)
         dp = dot(values, gh[...], NT)
         p = probs[u]
         ds = (p.astype(jnp.float32) * (dp - dotT[0:1])).astype(jnp.bfloat16)
@@ -302,13 +386,13 @@
 
     for h in range(heads):
         mine = slice(h * tok, (h + 1) * tok)
-        dq_ref[:, h * HDIM:(h + 1) * HDIM] = (
-            dqT[:, mine] * (total[0:1, mine] * scale)).T.astype(jnp.bfloat16)
+        dq_ref[:, h * HDIM:(h + 1) * HDIM] = flip(
+            (dqT[:, mine] * (total[0:1, mine] * scale)).astype(jnp.bfloat16)).astype(jnp.bfloat16)
 
     @pl.when(plane == 0)
     def _():
         def fold_in(j):
-            u = (z // 2 + 1 + j) % (PAIRS // 2)
+            u = far_pair(j)
             x2_copy(u).wait_recv()
 
             @pl.when(u <= own_pair)
@@ -331,13 +415,13 @@
     acc[...] = pair[own_pair, z % 2].astype(jnp.float32)
 
     def z_land(s):
-        source = (z + s) % RING
-
-        @pl.when((plane == 0) | (source > z))
-        def _():
-            remote(zbuf.at[source], zbuf.at[source], send_z2.at[0], recv_z2.at[source],
-                   ctx=ctx_of(plane, source, core)).wait_recv()
-            acc[...] += zbuf[source].astype(jnp.float32)
+        sender = (z + s) % RING
+
+        @pl.when((plane == 0) | (sender > z))
+        def _():
+            remote(zbuf.at[sender], zbuf.at[sender], send_z2.at[0], recv_z2.at[sender],
+                   ctx=ctx_of(plane, sender, core)).wait_recv()
+            acc[...] += zbuf[sender].astype(jnp.float32)
 
     loop(1, RING, z_land)
     kg_ref[0] = acc[:, :HDIM].astype(jnp.bfloat16)
@@ -352,20 +436,39 @@
         o_copy(s).wait_send()
 
     loop(1, groups, exchanged)
-    ring_copy(ctx, 0, True).wait_send()
-    ring_copy(ctx, 6, False).wait_send()
-    loop(1, RING - 2, lambda i: f_copy(i).wait_send())
+    first_copy(1, True).wait_send()
+    first_copy(1, False).wait_send()
+    loop(1, RING - 2, lambda i: r_copy(1, i).wait_send())
+
+    @pl.when(plane == 0)
+    def _():
+        x_copy(1, 0).wait_send()
+
+    @pl.when(plane == 1)
+    def _():
+        first_copy(2, True).wait_send()
+        first_copy(2, False).wait_send()
+        loop(1, RING - 2, lambda i: r_copy(2, i).wait_send())
 
     def gathered(i):
-        s_copy(plane, i).wait_send()
+        @pl.when((i >= 1) & goes(i))
+        def _():
+            f_copy(i).wait_send()
+
+        @pl.when(comes(i))
+        def _():
+            s_copy(0, plane, i).wait_send()
+
+        s_copy(1, plane, i).wait_send()
 
         @pl.when(plane == 0)
         def _():
-            x_copy(i).wait_send()
+            x_copy(0, i).wait_send()
 
         @pl.when(plane == 1)
         def _():
-            s_copy(0, i).wait_send()
+            s_copy(0, 0, i).wait_send()
+            s_copy(1, 0, i).wait_send()
 
         @pl.when((i < z) | ((plane == 0) & (i != z)))
         def _():
@@ -377,6 +480,13 @@
 
     loop(0, RING, gathered)
     loop(0, own_pair + 1, lambda i: s2_copy(pair_at(i)).wait_send())
+
+
+def hand_over(moved_in, dq_in, kg_in, vg_in, moved_out, dq_out, kg_out, vg_out):
+    moved_out[...] = moved_in[...]
+    dq_out[...] = dq_in[...]
+    kg_out[...] = kg_in[...]
+    vg_out[...] = vg_in[...]
 
 
 def per_device(queries, key_states, value_states, doc_start, move_plan, out_grad):
@@ -406,7 +516,9 @@
         in_specs=[vmem, vmem, vmem, vmem, smem, vmem],
         out_specs=(vmem,) * 4,
         scratch_shapes=[
-            pltpu.VMEM((pieces, tok, 2 * HDIM), bf),
+            pltpu.VMEM((pieces, tok, HDIM), bf),
+            pltpu.VMEM((pieces, tok, HDIM), bf),
+            pltpu.VMEM((tok, tok), bf),
             heads_bf, heads_bf, heads_bf, heads_bf,
             pltpu.VMEM((2 * PAIRS, tile, rows), f32),
             pltpu.VMEM((PAIRS, 2 * tile, rows), bf),
@@ -423,7 +535,7 @@
             pltpu.VMEM((PAIRS // 2, 2, tok, 2 * HDIM), bf),
             pltpu.VMEM((RING, tok, 2 * HDIM), bf),
             pltpu.VMEM((tok, 2 * HDIM), f32),
-            dma((RING,)), dma((RING,)), dma((2 * RING,)), dma((pieces,)),
+            dma((3, RING)), dma((2, RING)), dma((2, 2 * RING)), dma((2, pieces)),
             dma((groups,)), dma((groups,)), dma((groups,)), dma((groups,)),
             dma((PAIRS,)), dma((PAIRS,)), dma((PAIRS // 2,)), dma((PAIRS // 2,)),
             dma((RING,)), dma((RING,)),
@@ -434,6 +546,12 @@
         queries[0], key_states, value_states, doc_start, move_plan,
         out_grad.reshape(slots, block_rows, width),
     )
+    moved, dq, kg, vg = pl.pallas_call(
+        hand_over,
+        out_shape=tuple(jax.ShapeDtypeStruct(x.shape, x.dtype) for x in (moved, dq, kg, vg)),
+        in_specs=[vmem] * 4,
+        out_specs=(vmem,) * 4,
+    )(moved, dq, kg, vg)
     return moved.reshape(1, tok, width), dq[None], kg, vg
 
 

time: 76 us -> 74.3 us (0.978)
  local copies, waits for them, and re-layouts: 3.86 us -> 0 us
  Pallas kernels: 71.1 us -> 73.4 us
    unnamed x10 -> x0, local copies, waits for them, and re-layouts: 3.86 us -> none
    pallas_call x0 -> x1, Pallas kernels: none -> 1.85 us  [per_device(): pl.pallas_call(hand_over, out_shape=tuple((jax.ShapeDtypeStruct(x.shape,...]
where the time goes in v3:
time: 74.3 us; the launch traced here: 74 us
  Pallas kernels  73.4 us (99%)
    pallas_call x1, Pallas kernels, per_device(): pl.pallas_call(functools.partial(kernel, groups, slots, heads), out_shape...  71.5 us
    pallas_call x1, Pallas kernels, per_device(): pl.pallas_call(hand_over, out_shape=tuple((jax.ShapeDtypeStruct(x.shape,...  1.85 us

profile of v3, /device:TPU:1, one launch (start us, length us, event | category | flops | bytes accessed | tf_op | source)
XLA Modules:
  0.0 74.0 jit_solution(17918933348719034246)
XLA Ops:
  0.6 71.5 %shard_map.93 = (bf16[8,16,1024]{2,1,0:T(8,128)(2,1)}, bf16[128,1024]{1,0:T(8,128)(2,1)}, bf16[1,128,128]{2,1,0:T(8,128)(2,1)}, bf16[1,128,128]{2,1,0:T(8,128)(2,1)}) custom-call(bf16[128,1024]{1,0:T(8,128)(2,1)} %bitcast.4, bf16[1,128,128]{2,1,0:T(8,128)(2,1)} %k_ref.1, bf16[1,128,128]{2,1,0:T(8,128)(2,1)} %v_ref.1, s32[1,128]{1,0:T(1,128)} %starts_ref.1, ...), custom_call_target="tpu_custom_call" | custom-call | tf_op jit(solution)/shard_map/pallas_call | solution.py:508
  72.2 1.9 %shard_map.94 = (bf16[8,16,1024]{2,1,0:T(8,128)(2,1)}, bf16[128,1024]{1,0:T(8,128)(2,1)}, bf16[1,128,128]{2,1,0:T(8,128)(2,1)}, bf16[1,128,128]{2,1,0:T(8,128)(2,1)}) custom-call(bf16[8,16,1024]{2,1,0:T(8,128)(2,1)} %get-tuple-element.12.moved_in, bf16[128,1024]{1,0:T(8,128)(2,1)} %get-tuple-element.13.dq_in, bf16[1,128,128]{2,1,0:T(8,128)(2,1)} %get-tuple-element.14.kg_in, ...), custom_call_target="tpu_custom_call" | custom-call | tf_op jit(solution)/shard_map/pallas_call | solution.py:549

commit v4 on v3

--- a/solution.py
+++ b/solution.py
@@ -332,8 +332,9 @@
         return remote(part.at[u, 1 - core], sib.at[u], send_s2.at[u], recv_s2.at[u],
                       ctx=ctx_of(plane, z, 1 - core))
 
-    def x2_copy(u):
-        return remote(pair.at[u], xbuf.at[u], send_x2.at[u], recv_x2.at[u],
+    def x2_copy(spot):
+        u, which = spot // 2, spot % 2
+        return remote(pair.at[u, which], xbuf.at[u, which], send_x2.at[spot], recv_x2.at[spot],
                       ctx=ctx_of(1 - plane, z, core))
 
     def z2_copy(spot):
@@ -361,7 +362,8 @@
 
         @pl.when(u < far)
         def _():
-            x2_copy(u).start()
+            x2_copy(2 * u).start()
+            x2_copy(2 * u + 1).start()
 
         @pl.when((plane == 1) & (u >= far))
         def _():
@@ -393,18 +395,17 @@
     def _():
         def fold_in(j):
             u = far_pair(j)
-            x2_copy(u).wait_recv()
-
-            @pl.when(u <= own_pair)
-            def _():
-                pair[u] = add(pair[u], xbuf[u])
-
-            @pl.when(u > own_pair)
-            def _():
-                pair[u] = xbuf[u]
-
             for which in range(2):
                 spot = u * 2 + which
+                x2_copy(spot).wait_recv()
+
+                @pl.when(u <= own_pair)
+                def _():
+                    pair[u, which] = add(pair[u, which], xbuf[u, which])
+
+                @pl.when(u > own_pair)
+                def _():
+                    pair[u, which] = xbuf[u, which]
 
                 @pl.when(spot != z)
                 def _():
@@ -474,7 +475,7 @@
         def _():
             z2_copy(i).wait_send()
 
-        @pl.when(i < far)
+        @pl.when(plane == 1)
         def _():
             x2_copy(i).wait_send()
 
@@ -537,7 +538,7 @@
             pltpu.VMEM((tok, 2 * HDIM), f32),
             dma((3, RING)), dma((2, RING)), dma((2, 2 * RING)), dma((2, pieces)),
             dma((groups,)), dma((groups,)), dma((groups,)), dma((groups,)),
-            dma((PAIRS,)), dma((PAIRS,)), dma((PAIRS // 2,)), dma((PAIRS // 2,)),
+            dma((PAIRS,)), dma((PAIRS,)), dma((RING,)), dma((RING,)),
             dma((RING,)), dma((RING,)),
         ],
         compiler_params=pltpu.CompilerParams(

time: 74.3 us -> 73.2 us (0.985)
  Pallas kernels: 73.4 us -> 72.4 us
    pallas_call x1, Pallas kernels: 71.5 us -> 70.6 us  [per_device(): pl.pallas_call(functools.partial(kernel, groups, slots, heads), out_shape...]
where the time goes in v4:
time: 73.2 us; the launch traced here: 73.1 us
  Pallas kernels  72.4 us (99%)
    pallas_call x1, Pallas kernels, per_device(): pl.pallas_call(functools.partial(kernel, groups, slots, heads), out_shape...  70.6 us
    pallas_call x1, Pallas kernels, per_device(): pl.pallas_call(hand_over, out_shape=tuple((jax.ShapeDtypeStruct(x.shape,...  1.85 us

profile of v4, /device:TPU:1, one launch (start us, length us, event | category | flops | bytes accessed | tf_op | source)
XLA Modules:
  0.0 73.1 jit_solution(6466548136412489144)
XLA Ops:
  0.6 70.6 %shard_map.93 = (bf16[8,16,1024]{2,1,0:T(8,128)(2,1)}, bf16[128,1024]{1,0:T(8,128)(2,1)}, bf16[1,128,128]{2,1,0:T(8,128)(2,1)}, bf16[1,128,128]{2,1,0:T(8,128)(2,1)}) custom-call(bf16[128,1024]{1,0:T(8,128)(2,1)} %bitcast.4, bf16[1,128,128]{2,1,0:T(8,128)(2,1)} %k_ref.1, bf16[1,128,128]{2,1,0:T(8,128)(2,1)} %v_ref.1, s32[1,128]{1,0:T(1,128)} %starts_ref.1, ...), custom_call_target="tpu_custom_call" | custom-call | tf_op jit(solution)/shard_map/pallas_call | solution.py:509
  71.2 1.9 %shard_map.94 = (bf16[8,16,1024]{2,1,0:T(8,128)(2,1)}, bf16[128,1024]{1,0:T(8,128)(2,1)}, bf16[1,128,128]{2,1,0:T(8,128)(2,1)}, bf16[1,128,128]{2,1,0:T(8,128)(2,1)}) custom-call(bf16[8,16,1024]{2,1,0:T(8,128)(2,1)} %get-tuple-element.12.moved_in, bf16[128,1024]{1,0:T(8,128)(2,1)} %get-tuple-element.13.dq_in, bf16[1,128,128]{2,1,0:T(8,128)(2,1)} %get-tuple-element.14.kg_in, ...), custom_call_target="tpu_custom_call" | custom-call | tf_op jit(solution)/shard_map/pallas_call | solution.py:550

commit v5 on v4

--- a/solution.py
+++ b/solution.py
@@ -107,39 +107,20 @@
     dqT[...] = jnp.zeros_like(dqT)
     pl.semaphore_wait(barrier, groups - 1 + RING - 1 + 2)
 
-    def offset(i):
-        return jnp.where(i == 0, 0, jnp.where(i % 2 == 1, RING // 2 + i // 2, RING // 2 - i // 2))
-
     def origin(i):
-        return (z + RING - offset(i)) % RING
-
-    def goes(i):
-        return (plane == 0) | ((z + offset(i)) % RING >= z // 2 * 2)
-
-    def comes(i):
-        return (plane == 0) | (origin(i) <= z // 2 * 2 + 1)
-
-    def around(i):
         hop = (i + 1) // 2
         return (z + jnp.where(i % 2 == 1, RING - hop, hop)) % RING
 
     def stream(kind):
         return (keys_all, 0) if kind == 0 else (values_all, 1)
 
-    def source(kind, i):
-        return origin(i) if kind == 0 else around(i)
-
-    def f_copy(i):
-        return remote(keys_all.at[ctx], keys_all.at[ctx], send_f.at[0, i], recv_kv.at[0, ctx],
-                      ctx=ctx_of(plane, (z + offset(i)) % RING, core))
-
     def ring_copy(kind, i, sem, ahead):
-        block = ctx_of(0 if kind == 2 else plane, around(i), core)
-        return remote(values_all.at[block], values_all.at[block], send_f.at[kind, sem],
-                      recv_kv.at[1, block],
+        buf, which = stream(kind)
+        block = ctx_of(0 if kind == 2 else plane, origin(i), core)
+        return remote(buf.at[block], buf.at[block], send_f.at[kind, sem], recv_kv.at[which, block],
                       ctx=ctx_of(plane, (z + jnp.where(ahead, 1, RING - 1)) % RING, core))
 
-    def r_copy(kind, i):
+    def f_copy(kind, i):
         return ring_copy(kind, i, i, i % 2 == 1)
 
     def first_copy(kind, ahead):
@@ -147,13 +128,13 @@
 
     def x_copy(kind, i):
         buf, which = stream(kind)
-        block = ctx_of(0, source(kind, i), core)
+        block = ctx_of(0, origin(i), core)
         return remote(buf.at[block], buf.at[block], send_x.at[which, i], recv_kv.at[which, block],
                       ctx=ctx_of(1, z, core))
 
     def s_copy(kind, owner, i):
         buf, which = stream(kind)
-        block = ctx_of(owner, source(kind, i), core)
+        block = ctx_of(owner, origin(i), core)
         return remote(buf.at[block], buf.at[block], send_s.at[which, owner * RING + i],
                       recv_kv.at[which, block], ctx=ctx_of(plane, z, 1 - core))
 
@@ -171,20 +152,15 @@
                ctx=ctx_of(plane, z, 1 - core)).wait_recv()
 
     for kind in range(2):
+        first_copy(kind, True).start()
+        first_copy(kind, False).start()
+
+        @pl.when(plane == 0)
+        def _():
+            x_copy(kind, 0).start()
+
         s_copy(kind, plane, 0).start()
 
-        @pl.when(plane == 0)
-        def _():
-            x_copy(kind, 0).start()
-
-    def spread_out(i):
-        @pl.when(goes(i))
-        def _():
-            f_copy(i).start()
-
-    loop(1, RING, spread_out)
-    first_copy(1, True).start()
-    first_copy(1, False).start()
     loop(1, groups, lambda s: g_copy(s).start())
 
     def fold(x):
@@ -204,49 +180,41 @@
     def gather_step(i):
         @pl.when((i >= 1) & (i < RING))
         def _():
-            @pl.when(comes(i))
-            def _():
-                arrived(0, ctx_of(plane, origin(i), core))
-
-                @pl.when(plane == 0)
+            for kind in range(2):
+                arrived(kind, ctx_of(plane, origin(i), core))
+
+                @pl.when(i < RING - 2)
                 def _():
-                    x_copy(0, i).start()
-
-                s_copy(0, plane, i).start()
-
-            arrived(1, ctx_of(plane, around(i), core))
-
-            @pl.when(i < RING - 2)
-            def _():
-                r_copy(1, i).start()
-
-            s_copy(1, plane, i).start()
+                    f_copy(kind, i).start()
+
+                if kind == 0:
+                    @pl.when(plane == 0)
+                    def _():
+                        x_copy(0, i).start()
+
+                s_copy(kind, plane, i).start()
 
         @pl.when((plane == 1) & (i >= 1) & (i <= RING))
         def _():
             j = i - 1
-            arrived(0, ctx_of(0, origin(j), core))
-            s_copy(0, 0, j).start()
-            arrived(1, ctx_of(0, around(j), core))
-
-            @pl.when(j == 0)
-            def _():
-                first_copy(2, True).start()
-                first_copy(2, False).start()
-
-            @pl.when((j >= 1) & (j < RING - 2))
-            def _():
-                r_copy(2, j).start()
-
-            s_copy(1, 0, j).start()
+            for kind in (0, 2):
+                arrived(kind, ctx_of(0, origin(j), core))
+                if kind == 2:
+                    @pl.when(j == 0)
+                    def _():
+                        first_copy(2, True).start()
+                        first_copy(2, False).start()
+
+                    @pl.when((j >= 1) & (j < RING - 2))
+                    def _():
+                        f_copy(2, j).start()
+
+                s_copy(kind, 0, j).start()
 
         @pl.when((i >= 1) & (i <= RING))
         def _():
             near = plane * RING + origin(i - 1)
-
-            @pl.when(comes(i - 1))
-            def _():
-                arrived(0, CORES * near + 1 - core)
+            arrived(0, CORES * near + 1 - core)
 
             @pl.when(near <= 2 * own_pair + 1)
             def _():
@@ -416,13 +384,13 @@
     acc[...] = pair[own_pair, z % 2].astype(jnp.float32)
 
     def z_land(s):
-        sender = (z + s) % RING
-
-        @pl.when((plane == 0) | (sender > z))
-        def _():
-            remote(zbuf.at[sender], zbuf.at[sender], send_z2.at[0], recv_z2.at[sender],
-                   ctx=ctx_of(plane, sender, core)).wait_recv()
-            acc[...] += zbuf[sender].astype(jnp.float32)
+        source = (z + s) % RING
+
+        @pl.when((plane == 0) | (source > z))
+        def _():
+            remote(zbuf.at[source], zbuf.at[source], send_z2.at[0], recv_z2.at[source],
+                   ctx=ctx_of(plane, source, core)).wait_recv()
+            acc[...] += zbuf[source].astype(jnp.float32)
 
     loop(1, RING, z_land)
     kg_ref[0] = acc[:, :HDIM].astype(jnp.bfloat16)
@@ -437,9 +405,10 @@
         o_copy(s).wait_send()
 
     loop(1, groups, exchanged)
-    first_copy(1, True).wait_send()
-    first_copy(1, False).wait_send()
-    loop(1, RING - 2, lambda i: r_copy(1, i).wait_send())
+    for kind in range(2):
+        first_copy(kind, True).wait_send()
+        first_copy(kind, False).wait_send()
+        loop(1, RING - 2, lambda i: f_copy(kind, i).wait_send())
 
     @pl.when(plane == 0)
     def _():
@@ -449,18 +418,11 @@
     def _():
         first_copy(2, True).wait_send()
         first_copy(2, False).wait_send()
-        loop(1, RING - 2, lambda i: r_copy(2, i).wait_send())
+        loop(1, RING - 2, lambda i: f_copy(2, i).wait_send())
 
     def gathered(i):
-        @pl.when((i >= 1) & goes(i))
-        def _():
-            f_copy(i).wait_send()
-
-        @pl.when(comes(i))
-        def _():
-            s_copy(0, plane, i).wait_send()
-
-        s_copy(1, plane, i).wait_send()
+        for kind in range(2):
+            s_copy(kind, plane, i).wait_send()
 
         @pl.when(plane == 0)
         def _():

time: 73.2 us -> 71.7 us (0.980)
  Pallas kernels: 72.4 us -> 70.9 us
    pallas_call x1, Pallas kernels: 70.6 us -> 69 us  [per_device(): pl.pallas_call(functools.partial(kernel, groups, slots, heads), out_shape...]
where the time goes in v5:
time: 71.7 us; the launch traced here: 71.5 us
  Pallas kernels  70.9 us (99%)
    pallas_call x1, Pallas kernels, per_device(): pl.pallas_call(functools.partial(kernel, groups, slots, heads), out_shape...  69 us
    pallas_call x1, Pallas kernels, per_device(): pl.pallas_call(hand_over, out_shape=tuple((jax.ShapeDtypeStruct(x.shape,...  1.85 us

profile of v5, /device:TPU:1, one launch (start us, length us, event | category | flops | bytes accessed | tf_op | source)
XLA Modules:
  0.0 71.5 jit_solution(13436417875931816138)
XLA Ops:
  0.6 69.0 %shard_map.93 = (bf16[8,16,1024]{2,1,0:T(8,128)(2,1)}, bf16[128,1024]{1,0:T(8,128)(2,1)}, bf16[1,128,128]{2,1,0:T(8,128)(2,1)}, bf16[1,128,128]{2,1,0:T(8,128)(2,1)}) custom-call(bf16[128,1024]{1,0:T(8,128)(2,1)} %bitcast.4, bf16[1,128,128]{2,1,0:T(8,128)(2,1)} %k_ref.1, bf16[1,128,128]{2,1,0:T(8,128)(2,1)} %v_ref.1, s32[1,128]{1,0:T(1,128)} %starts_ref.1, ...), custom_call_target="tpu_custom_call" | custom-call | tf_op jit(solution)/shard_map/pallas_call | solution.py:471
  69.7 1.9 %shard_map.94 = (bf16[8,16,1024]{2,1,0:T(8,128)(2,1)}, bf16[128,1024]{1,0:T(8,128)(2,1)}, bf16[1,128,128]{2,1,0:T(8,128)(2,1)}, bf16[1,128,128]{2,1,0:T(8,128)(2,1)}) custom-call(bf16[8,16,1024]{2,1,0:T(8,128)(2,1)} %get-tuple-element.12.moved_in, bf16[128,1024]{1,0:T(8,128)(2,1)} %get-tuple-element.13.dq_in, bf16[1,128,128]{2,1,0:T(8,128)(2,1)} %get-tuple-element.14.kg_in, ...), custom_call_target="tpu_custom_call" | custom-call | tf_op jit(solution)/shard_map/pallas_call | solution.py:512

commit v6 on v5

--- a/solution.py
+++ b/solution.py
@@ -151,6 +151,7 @@
         remote(buf.at[block], buf.at[block], send_f.at[0, 0], recv_kv.at[which, block],
                ctx=ctx_of(plane, z, 1 - core)).wait_recv()
 
+    loop(1, groups, lambda s: g_copy(s).start())
     for kind in range(2):
         first_copy(kind, True).start()
         first_copy(kind, False).start()
@@ -161,7 +162,6 @@
 
         s_copy(kind, plane, 0).start()
 
-    loop(1, groups, lambda s: g_copy(s).start())
 
     def fold(x):
         return x.reshape(x.shape[0] // 8, 8, x.shape[1])

time: 71.7 us -> 74 us (1.032)
  Pallas kernels: 70.9 us -> 73.2 us
    pallas_call x1, Pallas kernels: 69 us -> 71.4 us  [per_device(): pl.pallas_call(functools.partial(kernel, groups, slots, heads), out_shape...]
where the time goes in v6:
time: 74 us; the launch traced here: 73.9 us
  Pallas kernels  73.2 us (99%)
    pallas_call x1, Pallas kernels, per_device(): pl.pallas_call(functools.partial(kernel, groups, slots, heads), out_shape...  71.4 us
    pallas_call x1, Pallas kernels, per_device(): pl.pallas_call(hand_over, out_shape=tuple((jax.ShapeDtypeStruct(x.shape,...  1.85 us

profile of v6, /device:TPU:1, one launch (start us, length us, event | category | flops | bytes accessed | tf_op | source)
XLA Modules:
  0.0 73.9 jit_solution(15999840955551917364)
XLA Ops:
  0.6 71.4 %shard_map.93 = (bf16[8,16,1024]{2,1,0:T(8,128)(2,1)}, bf16[128,1024]{1,0:T(8,128)(2,1)}, bf16[1,128,128]{2,1,0:T(8,128)(2,1)}, bf16[1,128,128]{2,1,0:T(8,128)(2,1)}) custom-call(bf16[128,1024]{1,0:T(8,128)(2,1)} %bitcast.4, bf16[1,128,128]{2,1,0:T(8,128)(2,1)} %k_ref.1, bf16[1,128,128]{2,1,0:T(8,128)(2,1)} %v_ref.1, s32[1,128]{1,0:T(1,128)} %starts_ref.1, ...), custom_call_target="tpu_custom_call" | custom-call | tf_op jit(solution)/shard_map/pallas_call | solution.py:471
  72.0 1.9 %shard_map.94 = (bf16[8,16,1024]{2,1,0:T(8,128)(2,1)}, bf16[128,1024]{1,0:T(8,128)(2,1)}, bf16[1,128,128]{2,1,0:T(8,128)(2,1)}, bf16[1,128,128]{2,1,0:T(8,128)(2,1)}) custom-call(bf16[8,16,1024]{2,1,0:T(8,128)(2,1)} %get-tuple-element.12.moved_in, bf16[128,1024]{1,0:T(8,128)(2,1)} %get-tuple-element.13.dq_in, bf16[1,128,128]{2,1,0:T(8,128)(2,1)} %get-tuple-element.14.kg_in, ...), custom_call_target="tpu_custom_call" | custom-call | tf_op jit(solution)/shard_map/pallas_call | solution.py:512
